TPU v7x, 32 devices: a whole 2x2x4 slice. The times are simulated.
32 devices in a mesh: gy: 4 (over z), gx: 8 (over y, x, core).
Axes of the slice: x: 2, y: 2, z: 4, core: 2. Of those that a mesh axis runs over, the one named last changes fastest.
Arguments:
- source_field: float32 [2, 1, 4096, 4096], P(None, None, 'gx', 'gy'), may hold values from -5 to 5
- receiver_field: float32 [2, 1, 4096, 4096], P(None, None, 'gx', 'gy'), may hold values from -5 to 5
- velocity_index: int32 [4, 4096, 4096], P(None, 'gx', 'gy'), may hold values from 0 to 63
- slowness: float32 [64], replicated, may hold values from 0.25 to 1
- freq_index: int32 [1], replicated, may hold values from 8 to 511
- root_modulus: float32 [1], replicated, may hold values from 0.9 to 1, as said below
- root_angle: float32 [1], replicated, may hold values from -3.140625 to 3.140625
Outputs:
- image: float32 [4, 4096, 4096], P(None, 'gx', 'gy')
- source_bottom: float32 [2, 1, 4096, 4096], P(None, None, 'gx', 'gy')
- receiver_top: float32 [2, 1, 4096, 4096], P(None, None, 'gx', 'gy')
Inputs may be any that keep to these rules, and one draw needn't show every extreme that they name: `root_modulus`: each modulus lies strictly below 1.
All inputs are finite; a program needn't handle non-finite values.
Results may differ from a plain program's by a relative error of at most 0.0003.
Values sent between devices are 32-bit elements; how exact they have to be, the bound alone decides.
No kernel may reach another device: no remote copies, remote signals or barrier semaphores. Data moves between devices by JAX's collectives and lax.ppermute only.
A program may use at most 192 MiB of HBM per device.

v0:
```python
import functools

import jax
import jax.numpy as jnp
import numpy as np
from jax import lax
from jax.experimental import pallas as pl
from jax.experimental.pallas import tpu as pltpu
from jax.sharding import PartitionSpec as P

PHASE_UNIT = 0.05
W = 128
F32 = jnp.float32
BF16 = jnp.bfloat16
MIB = 1024 * 1024


def complex_mul(a, b):
    return (a[0] * b[0] - a[1] * b[1], a[0] * b[1] + a[1] * b[0])


def root_powers(modulus, angle, exponent):
    k = exponent.astype(F32)
    coarse = jnp.round(angle * 512.0)
    fine = angle - coarse * (1.0 / 512.0)
    steps = k * coarse
    turns = jnp.round(steps * np.float32(1.0 / 512.0 / (2.0 * np.pi)))
    spin = (steps * (1.0 / 512.0) - turns * 6.28125) - turns * np.float32(2.0 * np.pi - 6.28125)
    spin = spin + k * fine
    magnitude = jnp.exp(jnp.log(modulus) * k)
    return (magnitude * jnp.cos(spin), magnitude * jnp.sin(spin))


def sweep_factors(modulus, angle):
    sin, cos = jnp.sin(angle), jnp.cos(angle)
    gap = (1.0 - modulus) * (1.0 + modulus)
    re, im = modulus * cos, modulus * sin
    den_re, den_im = gap + 2.0 * im * im, -2.0 * re * im
    den_sq = den_re * den_re + den_im * den_im
    inv = (den_re / den_sq, -den_im / den_sq)
    diag = (re * re - im * im + gap * gap * inv[0], -2.0 * re * im + gap * gap * inv[1])
    root_inv = (re / (modulus * modulus), -im / (modulus * modulus))
    off = complex_mul((0.0 * im, 2.0 * gap * im), complex_mul(root_inv, inv))
    end = (-gap * gap * inv[0], -gap * gap * inv[1])
    return diag, off, end


def real_rows(pair):
    re, im = pair
    rows, n = re.shape
    nb = n // W
    first = jnp.stack([re.reshape(rows, nb, W), -im.reshape(rows, nb, W)], axis=2)
    second = jnp.stack([im.reshape(rows, nb, W), re.reshape(rows, nb, W)], axis=2)
    return jnp.stack([first, second], axis=1).reshape(2 * rows, 2 * n)


def spread_rows(pair):
    re, im = pair
    rows, n = re.shape
    nb = n // W
    first = jnp.stack([re.reshape(rows, nb, W), im.reshape(rows, nb, W)], axis=2)
    second = jnp.stack([-im.reshape(rows, nb, W), re.reshape(rows, nb, W)], axis=2)
    return jnp.stack([first, second], axis=1).reshape(2 * rows, 2 * n)


def pad_rows(x, rows):
    return jnp.pad(x, ((0, rows - x.shape[0]), (0, 0)))


def halves(x):
    hi = x.astype(BF16)
    return hi, (x - hi.astype(F32)).astype(BF16)


def rounded_halves(x):
    hi = lax.reduce_precision(x, exponent_bits=8, mantissa_bits=7)
    return hi.astype(BF16), (x - hi).astype(BF16)


def state_exponents(length):
    nb = length // W
    m = np.arange(length)
    rows, masks = [], []
    for b in range(nb):
        rows += [b * W - 1 - m, m - (b + 1) * W]
        masks += [m < b * W, m >= (b + 1) * W]
    rows += [length - 1 - m, m]
    masks += [m >= 0, m >= 0]
    return np.maximum(np.stack(rows), 0).astype(np.int32), np.stack(masks)


def state_matrix(modulus, angle, length):
    exps, masks = state_exponents(length)
    re, im = root_powers(modulus, angle, jnp.asarray(exps))
    masks = jnp.asarray(masks)
    return real_rows((jnp.where(masks, re, 0.0), jnp.where(masks, im, 0.0)))


def partner(mine, slot, count, way):
    if count & (count - 1) == 0:
        return mine ^ slot
    return (mine + way * slot) % count


def exchange(pieces, axis):
    count = len(pieces)
    got = [pieces[0]]
    for s in range(1, count):
        pairs = [(d, partner(d, s, count, 1)) for d in range(count)]
        got.append(lax.ppermute(pieces[s], axis, pairs))
    return got


def link_coefs(modulus, angle, off, end, count, mine, length):
    slots = np.arange(count, dtype=np.int32)
    root = (modulus * jnp.cos(angle), modulus * jnp.sin(angle))
    one = jnp.ones((count,), F32)
    zero = jnp.zeros((count,), F32)

    def factors(other):
        far = root_powers(modulus, angle, length * (2 * count - 2 - mine - other))
        near = root_powers(modulus, angle, length * jnp.maximum(jnp.abs(other - mine) - 1, 0))
        return near, complex_mul(end, far)

    other = partner(mine, slots, count, 1)
    near, tail = factors(other)
    head = complex_mul(complex_mul(off, root), near)
    before = other < mine
    send_f = (jnp.where(before, tail[0], one), jnp.where(before, tail[1], zero))
    send_b = (jnp.where(before, head[0], zero), jnp.where(before, head[1], zero))
    other = partner(mine, slots, count, -1)
    near, tail = factors(other)
    before, after = other < mine, other > mine
    recv_f = (jnp.where(before, near[0], zero), jnp.where(before, near[1], zero))
    recv_b = (jnp.where(after, one, tail[0]), jnp.where(after, zero, tail[1]))
    return jnp.stack([*send_f, *send_b, *recv_f, *recv_b])


def split3(x, first):
    hi, lo = halves(x)
    return jnp.concatenate([hi, lo, hi] if first else [hi, hi, lo], axis=0)


def nt(a, b):
    return lax.dot_general(a, b, (((1,), (1,)), ((), ())), preferred_element_type=F32)


def tn(a, b):
    return lax.dot_general(a, b, (((0,), (0,)), ((), ())), preferred_element_type=F32)


def nn(a, b):
    return lax.dot_general(a, b, (((1,), (0,)), ((), ())), preferred_element_type=F32)


def lookup(table, index):
    chunks = table.shape[0]
    out = None
    for c in range(chunks):
        row = jnp.broadcast_to(table[c : c + 1, :], index.shape)
        here = jnp.clip(index - c * W, 0, W - 1) if chunks > 1 else index
        got = jnp.take_along_axis(row, here, axis=1, mode="promise_in_bounds")
        out = got if out is None else jnp.where(index >= c * W, got, out)
    return out


def weigh(coef, row, col, pair):
    cr, ci = coef[col, row], coef[col + 1, row]
    return (cr * pair[0] - ci * pair[1], cr * pair[1] + ci * pair[0])


def add_pair(a, b):
    return b if a is None else (a[0] + b[0], a[1] + b[1])


def gather_entries(coef, recv, count, chain):
    first = second = None
    for e in range(count):
        pair = (recv[e][2 * chain : 2 * chain + 1, :], recv[e][2 * chain + 1 : 2 * chain + 2, :])
        first = add_pair(first, weigh(coef, e, 4, pair))
        second = add_pair(second, weigh(coef, e, 6, pair))
    return first, second


def write_pieces(coef, pieces, count, chain, f_pair, b_pair):
    for e in range(count):
        out = add_pair(weigh(coef, e, 0, f_pair), weigh(coef, e, 2, b_pair))
        pieces[e][2 * chain : 2 * chain + 1, :] = out[0]
        pieces[e][2 * chain + 1 : 2 * chain + 2, :] = out[1]


def put_turned(t_hi, t_lo, chain, a, b, pair):
    for part in range(2):
        hi, lo = halves(pair[part])
        t_hi[chain, a, b * W : (b + 1) * W, part * W : (part + 1) * W] = hi
        t_lo[chain, a, b * W : (b + 1) * W, part * W : (part + 1) * W] = lo


def add_states(acc, t_hi, t_lo, st, a, b):
    rows = slice(b * W, (b + 1) * W)
    high = jnp.concatenate([t_hi[0, a, rows, :], t_hi[1, a, rows, :]], axis=0)
    low = jnp.concatenate([t_lo[0, a, rows, :], t_lo[1, a, rows, :]], axis=0)
    part = nn(jnp.concatenate([high, low], axis=1), st[b])
    return part if acc is None else acc + part


def put_states(acc, coef_y, y_state, y_pieces, nby, county, a):
    half = acc.shape[1] // 2
    rows = y_state.shape[2]
    turned = acc.T
    both = turned[:rows] + turned[half : half + rows]
    d = 4 * nby
    for chain in range(2):
        total = both[:, chain * W : (chain + 1) * W]
        y_state[chain, a] = total
        places = [ref.at[:, a * W : (a + 1) * W] for ref in y_pieces]
        write_pieces(
            coef_y, places, county, chain,
            (total[d : d + 1], total[d + 1 : d + 2]), (total[d + 2 : d + 3], total[d + 3 : d + 4]),
        )


def first_kernel(nby, county, src, rec, idx, table, st, coef_y, early, t_hi, t_lo, y_state, *y_pieces):
    acc = None
    for b in range(nby):
        lanes = slice(b * W, (b + 1) * W)
        put_turned(t_hi, t_lo, 0, 0, b, (src[0, 0, :, lanes], src[1, 0, :, lanes]))
        index = idx[0, :, lanes]
        cos, sin = lookup(table[0], index), lookup(table[1], index)
        put_turned(t_hi, t_lo, 1, 0, b, complex_mul((rec[0, 0, :, lanes], -rec[1, 0, :, lanes]), (cos, sin)))
        acc = add_states(acc, t_hi, t_lo, st, 0, b)
    put_states(acc, coef_y, y_state, y_pieces, nby, county, 0)


def local_kernel(nbx, nby, levels, t_hi, t_lo, y_state, my3, sp_y, lx, *refs):
    count = len(levels)
    far, (w_out, x_state), near = refs[:count], refs[count : count + 2], refs[count + 2 : 2 * count + 2]
    vx_hi, vx_lo, sems = refs[2 * count + 2 :]
    copies = []
    for n, level in enumerate(levels):
        source = far[n] if level is None else far[n].at[level]
        copies.append(pltpu.make_async_copy(source, near[n], sems.at[n]))
        copies[-1].start()
    x_state[...] = jnp.zeros_like(x_state)

    def block(i, carry):
        c, a = i // nbx, i % nbx
        state = y_state[c, a]
        for j in range(0, nby, 2):
            rows = slice(j * W, (j + 2) * W)
            high, low = t_hi[c, a, rows, :], t_lo[c, a, rows, :]
            main = nn(jnp.concatenate([high, low, high], axis=1), my3[...])
            for b in (j, j + 1):
                v = main[(b - j) * W : (b - j + 1) * W] + tn(split3(state[4 * b : 4 * b + 4, :], True), sp_y[...])
                hi, lo = halves(v)
                for part in range(2):
                    at = slice(part * W, (part + 1) * W)
                    vx_hi[at, b * W : (b + 1) * W] = hi[:, at]
                    vx_lo[at, b * W : (b + 1) * W] = lo[:, at]
        left = lx[a]
        for j in range(0, nby, 2):
            lanes = slice(j * W, (j + 2) * W)
            high, low = vx_hi[:, lanes], vx_lo[:, lanes]
            out = nn(left, jnp.concatenate([high, low, high], axis=0))
            w_out[c, a, :, lanes] = out[: 2 * W]
            x_state[c, :, lanes] += out[2 * W :]
        return carry

    lax.fori_loop(0, 2 * nbx, block, 0)
    for copy in copies:
        copy.wait()


def link_kernel(nbx, county, countx, x_local, coef_y, coef_x, sx3, edge, my3, *refs):
    recv_y, (x_state, ym), x_pieces = refs[:county], refs[county : county + 2], refs[county + 2 :]
    cols = []
    for chain in range(2):
        (fr, fi), (br, bi) = gather_entries(coef_y, recv_y, county, chain)
        rows = [(fr, fi), (-fi, fr), (br, bi), (-bi, br)]
        for a in range(nbx):
            lanes = slice(a * W, (a + 1) * W)
            cols.append(jnp.concatenate([jnp.concatenate([p[:, lanes], q[:, lanes]], axis=1) for p, q in rows]
                                        + [jnp.zeros((4, 2 * W), F32)], axis=0))
    hi, lo = halves(jnp.concatenate(cols, axis=0))
    swept = nn(jnp.concatenate([hi, lo, hi], axis=1), my3[...])
    for chain in range(2):
        for a in range(nbx):
            at = 8 * (chain * nbx + a)
            ym[chain, :, 2 * W * a : 2 * W * (a + 1)] = swept[at : at + 8]
    lines = jnp.concatenate(
        [jnp.concatenate(cols[chain * nbx : (chain + 1) * nbx], axis=1) for chain in range(2)], axis=0
    )
    hi, lo = halves(lines)
    gains = nt(sx3[...], jnp.concatenate([hi, lo, hi], axis=1))
    for chain in range(2):
        total = x_local[chain]
        for s in range(4):
            total = total + gains[:, 8 * chain + s : 8 * chain + s + 1] * edge[s : s + 1, :]
        for a in range(nbx):
            x_state[chain, a, 0:4, :] = total[4 * a : 4 * a + 4, :]
            x_state[chain, a, 4:8, :] = jnp.zeros((4, total.shape[1]), F32)
        d = 4 * nbx
        write_pieces(
            coef_x, x_pieces, countx, chain,
            (total[d : d + 1], total[d + 1 : d + 2]), (total[d + 2 : d + 3], total[d + 3 : d + 4]),
        )


def post_kernel(plan, nbx, nby, county, countx, *refs):
    refs = list(refs)
    take = lambda: refs.pop(0)
    w_in, x_state, ym, coef_x, edge, sp_x, sp_dev, table = (take() for _ in range(8))
    recv_x = [take() for _ in range(countx)]
    idx_s = take()
    idx_r, st, coef_y = (take(), take(), take()) if plan["turn"] else (None,) * 3
    olds = [{"s": (take(), take()) if z[1] == "split" else take() if z[1] == "field" else None,
             "r": take() if z[2] else None} for z in plan["images"]]
    if plan["alias"]:
        take()
    if plan["turn"]:
        t_hi, t_lo, y_state = (take() for _ in range(3))
        y_pieces = [take() for _ in range(county)]
    else:
        src_out, rec_out = take(), take()
    keep_out = take() if plan["keep"] else None
    image = take() if plan["images"] else None
    src_part, rec_part = (None, None) if plan["turn"] else (take(), take())
    keep_part = take() if plan["keep"] else None
    image_part = take() if plan["images"] else None
    sems = take()
    copies = []

    def send(part, out):
        copies.append(pltpu.make_async_copy(part, out, sems.at[len(copies)]))
        copies[-1].start()

    entries = [gather_entries(coef_x, recv_x, countx, chain) for chain in range(2)]
    step = 2 if nby % 2 == 0 else 1
    chunks = [(a, b) for a in range(nbx) for b in range(0, nby, step)]
    stacks = {}

    def correction(a, start):
        if a not in stacks:
            stacks[a] = []
            for chain in range(2):
                first, second = entries[chain]
                right = jnp.concatenate([x_state[chain, a, 0:4, :], *first, *second, edge[0:4, :]], axis=0)
                left = jnp.concatenate(
                    [sp_x[...], sp_dev[a], ym[chain, 0:4, 2 * W * a : 2 * W * (a + 1)]], axis=0
                )
                stacks[a].append((split3(left, True), split3(right, False)))
        return [tn(left, right[:, start * W : (start + step) * W]) for left, right in stacks[a]]

    def finish(a, b):
        nonlocal acc
        if plan["turn"]:
            acc = add_states(acc if b else None, t_hi, t_lo, st, a, b)
            if b == nby - 1:
                put_states(acc, coef_y, y_state, y_pieces, nby, county, a)

    acc, before = None, None
    coming = correction(*chunks[0])
    for n_chunk, (a, start) in enumerate(chunks):
        place = slice(a * W, (a + 1) * W)
        fixes = coming
        if n_chunk + 1 < len(chunks):
            coming = correction(*chunks[n_chunk + 1])
        for b in range(start, start + step):
            lanes = slice(b * W, (b + 1) * W)
            fields = []
            for chain in range(2):
                u = w_in[chain, a, :, lanes] + fixes[chain][:, (b - start) * W : (b - start + 1) * W]
                fields.append((u[:W], u[W:]))
            index = idx_s[place, lanes]
            source = complex_mul(fields[0], (lookup(table[0], index), lookup(table[1], index)))
            back = fields[1]
            if plan["turn"]:
                put_turned(t_hi, t_lo, 0, a, b, source)
                index = idx_r[place, lanes]
                turn = (lookup(table[0], index), lookup(table[1], index))
                put_turned(t_hi, t_lo, 1, a, b, complex_mul(back, turn))
            else:
                src_part[a, 0, :, lanes], src_part[a, 1, :, lanes] = source
                rec_part[a, 0, :, lanes], rec_part[a, 1, :, lanes] = back[0], -back[1]
            if keep_out is not None:
                keep_part[a, 0, :, lanes], keep_part[a, 1, :, lanes] = back
            for n, (old, (_, how, has_r)) in enumerate(zip(olds, plan["images"])):
                if how == "split":
                    hi, lo = old["s"]
                    rows = slice(b * W, (b + 1) * W)
                    s = [hi[a, rows, p * W : (p + 1) * W].astype(F32) + lo[a, rows, p * W : (p + 1) * W].astype(F32)
                         for p in range(2)]
                elif how == "field":
                    s = (old["s"][0, 0, place, lanes], old["s"][1, 0, place, lanes])
                else:
                    s = source
                r = (old["r"][0, place, lanes], old["r"][1, place, lanes]) if has_r else back
                image_part[n, a, :, lanes] = s[0] * r[0] - s[1] * r[1]
            if before is not None:
                finish(*before)
            before = (a, b)
        if start + step < nby:
            continue
        if not plan["turn"]:
            send(src_part.at[a], src_out.at[:, 0, place])
            send(rec_part.at[a], rec_out.at[:, 0, place])
        if plan["keep"]:
            send(keep_part.at[a], keep_out.at[:, place])
        for n, (z, _, _) in enumerate(plan["images"]):
            send(image_part.at[n, a], image.at[z, place])
    finish(*before)
    for copy in copies:
        copy.wait()


def whole(shape):
    return pl.BlockSpec(shape, lambda *_: (0,) * len(shape))


SMEM = pl.BlockSpec(memory_space=pltpu.SMEM)
VMEM = pl.BlockSpec(memory_space=pltpu.VMEM)
ANY = pl.BlockSpec(memory_space=pl.ANY)


def in_hbm(x):
    return pltpu.with_memory_space_constraint(x, pltpu.HBM)


def params(mib):
    return pltpu.CompilerParams(vmem_limit_bytes=mib * MIB)


def on_device(source_field, receiver_field, velocity_index, slowness, freq_index, root_modulus, root_angle):
    depth, len_x, len_y = velocity_index.shape
    nbx, nby = len_x // W, len_y // W
    countx, county = lax.axis_size("gx"), lax.axis_size("gy")
    modulus, angle = root_modulus[0], root_angle[0]
    diag, off, end = sweep_factors(modulus, angle)

    entries = slowness.shape[0]
    chunks = -(-entries // W)
    rate = freq_index.astype(F32)[0] * PHASE_UNIT
    phase = jnp.pad(rate * slowness, (0, chunks * W - entries)).reshape(chunks, W)
    table = jnp.stack([jnp.cos(phase), jnp.sin(phase)])

    at = np.arange(W)
    dist = np.abs(at[:, None] - at[None, :]).astype(np.int32)
    pw = root_powers(modulus, angle, jnp.asarray(dist))
    pw = complex_mul(off, pw)
    on = jnp.asarray(dist == 0)
    mr, mi = jnp.where(on, diag[0], pw[0]), jnp.where(on, diag[1], pw[1])
    my = jnp.concatenate([jnp.concatenate([mr, mi], 1), jnp.concatenate([-mi, mr], 1)], 0)
    mx = jnp.concatenate([jnp.concatenate([mr, -mi], 1), jnp.concatenate([mi, mr], 1)], 0)
    my_hi, my_lo = rounded_halves(my)
    mx_hi, mx_lo = rounded_halves(mx)

    rows_y = -(-(4 * nby + 4) // 16) * 16
    rows_x = -(-(4 * nbx + 4) // 16) * 16
    st_hi, st_lo = rounded_halves(pad_rows(state_matrix(modulus, angle, len_y), -(-rows_y // 64) * 64))
    st = jnp.concatenate([jnp.concatenate([st_hi, st_lo], axis=0), jnp.concatenate([st_hi, 0 * st_lo], axis=0)], axis=1)
    st = st.reshape(st.shape[0], 2, nby, 2 * W).transpose(2, 1, 3, 0).reshape(nby, 4 * W, st.shape[0])
    sx = pad_rows(state_matrix(modulus, angle, len_x), rows_x)
    sx_hi, sx_lo = rounded_halves(sx)
    lx = jnp.concatenate([
        jnp.broadcast_to(jnp.concatenate([mx_hi, mx_hi, mx_lo], axis=1)[None], (nbx, 2 * W, 6 * W)),
        jnp.concatenate([x.reshape(rows_x, nbx, 2 * W).transpose(1, 0, 2) for x in (sx_hi, sx_hi, sx_lo)], axis=2),
    ], axis=1)
    my3 = jnp.concatenate([my_hi, my_hi, my_lo], axis=0)

    near = complex_mul(off, root_powers(modulus, angle, jnp.asarray(np.stack([at + 1, W - at]).astype(np.int32))))
    spread = spread_rows(near)
    sp_hi, sp_lo = rounded_halves(spread)
    sp_y = jnp.concatenate([sp_hi, sp_hi, sp_lo], axis=0)

    def edges(length):
        m = np.arange(length)
        ahead = complex_mul(off, root_powers(modulus, angle, jnp.asarray((m + 1).astype(np.int32))))
        behind = root_powers(modulus, angle, jnp.asarray((length - 1 - m).astype(np.int32)))
        return jnp.stack([ahead[0], behind[0]]), jnp.stack([ahead[1], behind[1]])

    edge_x = spread_rows(edges(len_x)).reshape(4, nbx, 2 * W).transpose(1, 0, 2)
    er, ei = edges(len_y)
    edge_y = jnp.concatenate([jnp.stack([er, ei], axis=1).reshape(4, len_y), jnp.zeros((4, len_y), F32)], axis=0)

    coef_y = link_coefs(modulus, angle, off, end, county, lax.axis_index("gy"), len_y)
    coef_x = link_coefs(modulus, angle, off, end, countx, lax.axis_index("gx"), len_x)

    sx3 = jnp.concatenate([sx_hi, sx_hi, sx_lo], axis=1)
    (my3, sp_y, lx, sx3, edge_y, spread, edge_x, table, st, coef_y, coef_x) = lax.optimization_barrier(
        (my3, sp_y, lx, sx3, edge_y, spread, edge_x, table, st, coef_y, coef_x)
    )

    turned = jax.ShapeDtypeStruct((2, nbx, nby * W, 2 * W), BF16)
    turned_spec = pl.BlockSpec((2, 1, nby * W, 2 * W), lambda a: (0, a, 0, 0))
    y_state_shape = jax.ShapeDtypeStruct((2, nbx, rows_y, W), F32)
    y_state_spec = pl.BlockSpec((2, 1, rows_y, W), lambda a: (0, a, 0, 0))
    y_piece_shape = jax.ShapeDtypeStruct((4, len_x), F32)
    y_piece_spec = pl.BlockSpec((4, W), lambda a: (0, a))
    field_spec = pl.BlockSpec((2, 1, W, len_y), lambda a: (0, 0, a, 0))
    level_spec = lambda z: pl.BlockSpec((1, W, len_y), lambda a: (z, a, 0))
    turn_out = [turned, turned, y_state_shape] + [y_piece_shape] * county
    turn_specs = [turned_spec, turned_spec, y_state_spec] + [y_piece_spec] * county

    t_hi, t_lo, y_state, *y_pieces = pl.pallas_call(
        functools.partial(first_kernel, nby, county),
        grid=(nbx,),
        in_specs=[field_spec, field_spec, level_spec(depth - 1), whole(table.shape), whole(st.shape), SMEM, ANY],
        out_specs=turn_specs,
        out_shape=turn_out,
        compiler_params=params(20),
        name="first",
    )(in_hbm(source_field), in_hbm(receiver_field), in_hbm(velocity_index), table, st, coef_y, my3)

    def local(t_hi, t_lo, y_state, ahead):
        shapes = [x.shape if level is None else x.shape[1:] for x, level in ahead]
        return pl.pallas_call(
            functools.partial(local_kernel, nbx, nby, tuple(level for _, level in ahead)),
            in_specs=[VMEM] * 6 + [ANY] * len(ahead),
            out_specs=[VMEM] * (2 + len(ahead)),
            out_shape=[
                jax.ShapeDtypeStruct((2, nbx, 2 * W, len_y), F32),
                jax.ShapeDtypeStruct((2, rows_x, len_y), F32),
            ] + [jax.ShapeDtypeStruct(shape, x.dtype) for (x, _), shape in zip(ahead, shapes)],
            scratch_shapes=[pltpu.VMEM((2 * W, len_y), BF16)] * 2 + [pltpu.SemaphoreType.DMA((len(ahead),))],
            compiler_params=params(8),
            name="local",
        )(t_hi, t_lo, y_state, my3, sp_y, lx, *[in_hbm(x) for x, _ in ahead])

    link = pl.pallas_call(
        functools.partial(link_kernel, nbx, county, countx),
        in_specs=[VMEM] + [SMEM] * 2 + [VMEM] * (3 + county),
        out_specs=[VMEM] * (2 + countx),
        out_shape=[
            jax.ShapeDtypeStruct((2, nbx, 8, len_y), F32),
            jax.ShapeDtypeStruct((2, 8, 2 * len_x), F32),
        ] + [jax.ShapeDtypeStruct((4, len_y), F32)] * countx,
        compiler_params=params(8),
        name="link",
    )

    source_levels = {0: ("field", (source_field,))}
    kept = {}
    image = None
    for step in range(depth):
        turn = step < depth - 1
        level_r = depth - 1 - step
        todo = [z for z in range(depth) if max(z - 1, depth - 1 - z) == step]
        plan = {
            "turn": turn,
            "keep": level_r - 1 > step,
            "images": [(z, None if z - 1 == step else source_levels[z][0], z != level_r) for z in todo],
            "alias": bool(todo) and image is not None,
        }
        ahead = [(velocity_index, step)] + ([(velocity_index, depth - 2 - step)] if turn else [])
        for z, how, has_r in plan["images"]:
            if how == "split":
                ahead += [(x, 0) for x in source_levels[z][1]]
            elif how == "field":
                ahead += [(x, None) for x in source_levels[z][1]]
            if has_r:
                ahead += [(kept[z], None)]
        w, x_local, *fetched = local(t_hi, t_lo, y_state, ahead)
        recv_y = exchange(y_pieces, "gy")
        x_state, ym, *x_pieces = link(x_local, coef_y, coef_x, sx3, edge_y, my3, *recv_y)
        recv_x = exchange(x_pieces, "gx")
        args = [w, x_state, ym, coef_x, edge_y, spread, edge_x, table, *recv_x, fetched.pop(0)]
        specs = [VMEM] * 3 + [SMEM] + [VMEM] * (5 + countx)
        if turn:
            args += [fetched.pop(0), st, coef_y]
            specs += [VMEM, VMEM, SMEM]
        args += fetched
        specs += [VMEM] * len(fetched)
        aliases, scratch, sends = {}, [], 0
        if turn:
            shapes, out_specs = list(turn_out), [VMEM] * len(turn_out)
        else:
            shapes = [pltpu.HBM(source_field.shape, F32)] * 2
            out_specs = [ANY] * 2
            scratch += [pltpu.VMEM((nbx, 2, W, len_y), F32)] * 2
            sends += 2
        if plan["keep"]:
            shapes.append(pltpu.HBM((2, len_x, len_y), F32))
            out_specs.append(ANY)
            scratch += [pltpu.VMEM((nbx, 2, W, len_y), F32)]
            sends += 1
        if todo:
            if plan["alias"]:
                aliases = {len(args): len(shapes)}
                args += [in_hbm(image)]
                specs += [ANY]
            shapes.append(pltpu.HBM((depth, len_x, len_y), F32))
            out_specs.append(ANY)
            scratch += [pltpu.VMEM((len(todo), nbx, W, len_y), F32)]
            sends += len(todo)
        outs = pl.pallas_call(
            functools.partial(post_kernel, plan, nbx, nby, county, countx),
            in_specs=specs,
            out_specs=out_specs,
            out_shape=shapes,
            scratch_shapes=scratch + [pltpu.SemaphoreType.DMA((max(sends, 1) * nbx,))],
            input_output_aliases=aliases,
            compiler_params=params(20),
            name="post",
        )(*args)
        outs = list(outs)
        if turn:
            t_hi, t_lo, y_state, *y_pieces = outs[: 3 + county]
            outs = outs[3 + county :]
            source_levels[step + 1] = ("split", (t_hi, t_lo))
        else:
            source, receiver = outs[:2]
            outs = outs[2:]
        if plan["keep"]:
            kept[level_r] = outs.pop(0)
        if todo:
            image = outs.pop(0)
    return image, source, receiver


def solution(mesh):
    placed = (
        P(None, None, "gx", "gy"),
        P(None, None, "gx", "gy"),
        P(None, "gx", "gy"),
        P(),
        P(),
        P(),
        P(),
    )
    return jax.shard_map(
        on_device,
        mesh=mesh,
        in_specs=placed,
        out_specs=(P(None, "gx", "gy"), P(None, None, "gx", "gy"), P(None, None, "gx", "gy")),
        check_vma=False,
    )
```

profile of v0, /device:TPU:0, one launch (start us, length us, event | category | flops | bytes accessed | tf_op | source)
XLA Modules:
  0.0 160.4 jit_solution(17805772946151074469)
XLA Ops:
  2.4 0.7 fusion.60
  3.2 1.3 multiply_select_fusion
  5.5 0.6 select_bitcast_fusion.1
  6.2 0.6 select_bitcast_fusion.7
  9.8 0.6 fusion.56
  11.5 0.6 select_bitcast_fusion.5
  13.1 1.2 copy.38
  14.5 1.1 fusion.61
  16.5 7.4 %first.1 = (bf16[2,4,1024,256]{3,2,1,0:T(8,128)(2,1)S(1)}, bf16[2,4,1024,256]{3,2,1,0:T(8,128)(2,1)S(1)}, f32[2,4,48,128]{3,2,1,0:T(8,128)S(1)}, f32[4,512]{1,0:...) custom-call(f32[2,1,512,1024]{3,2,1,0:T(8,128)} %refs_1_.7, ...), custom_call_target="tpu_custom_call" | custom-call | tf_op jit(solution)/shard_map/first/pallas_call | solution.py:504
  23.9 3.1 %collective-permute-start = (f32[4,512]{1,0:T(4,128)S(1)}, f32[4,512]{1,0:T(4,128)S(1)}, u32[]{:S(2)}, u32[]{:S(2)}) collective-permute-start(f32[4,512]{1,0:T(4,128)S(1)} %get-tuple-element.122), channel_id=1, source_target_pairs={{0,8},{8,0},{16,24},{24,16},{1,9},{9,1},{17,25},{25,17},{2,10},{10... | collective-permute-start | bytes 24584 | tf_op jit(solution)/shard_map/ppermute | solution.py:110
  27.0 2.6 %collective-permute-start.1 = (f32[4,512]{1,0:T(4,128)S(1)}, f32[4,512]{1,0:T(4,128)S(1)}, u32[]{:S(2)}, u32[]{:S(2)}) collective-permute-start(f32[4,512]{1,0:T(4,128)S(1)} %get-tuple-element.123), channel_id=1, source_target_pairs={{0,16},{8,24},{16,0},{24,8},{1,17},{9,25},{17,1},{25,9},{2,18},{10... | collective-permute-start | bytes 24584 | tf_op jit(solution)/shard_map/ppermute | solution.py:110
  29.6 9.7 %local.4 = (f32[2,4,256,1024]{3,2,1,0:T(8,128)S(1)}, f32[2,32,1024]{2,1,0:T(8,128)S(1)}, s32[512,1024]{1,0:T(8,128)S(1)}, s32[512,1024]{1,0:T(8,128)S(1)}) custom-call(bf16[2,4,1024,256]{3,2,1,0:T(8,128)(2,1)S(1)} %get-tuple-element.111.t_hi, bf16[2,4,1024,256]{3,2,1,0:T(8,128)(2,1)S(1)} %get-tuple-element.112.t_lo, ...), custom_call_target="tpu_custom_call" | custom-call | tf_op jit(solution)/shard_map/local/pallas_call | solution.py:516
  39.3 1.4 link.4
  40.8 1.8 %collective-permute-start.4 = (f32[4,1024]{1,0:T(4,128)S(1)}, f32[4,1024]{1,0:T(4,128)S(1)}, u32[]{:S(2)}, u32[]{:S(2)}) collective-permute-start(f32[4,1024]{1,0:T(4,128)S(1)} %get-tuple-element.131), channel_id=1, source_target_pairs={{0,2},{1,3},{2,0},{3,1},{4,6},{5,7},{6,4},{7,5},{8,10},{9,11},{10,... | collective-permute-start | bytes 49160 | tf_op jit(solution)/shard_map/ppermute | solution.py:110
  42.7 1.8 %collective-permute-start.6 = (f32[4,1024]{1,0:T(4,128)S(1)}, f32[4,1024]{1,0:T(4,128)S(1)}, u32[]{:S(2)}, u32[]{:S(2)}) collective-permute-start(f32[4,1024]{1,0:T(4,128)S(1)} %get-tuple-element.133), channel_id=1, source_target_pairs={{0,4},{1,5},{2,6},{3,7},{4,0},{5,1},{6,2},{7,3},{8,12},{9,13},{10,... | collective-permute-start | bytes 49160 | tf_op jit(solution)/shard_map/ppermute | solution.py:110
  44.4 2.6 %collective-permute-start.8 = (f32[4,1024]{1,0:T(4,128)S(1)}, f32[4,1024]{1,0:T(4,128)S(1)}, u32[]{:S(2)}, u32[]{:S(2)}) collective-permute-start(f32[4,1024]{1,0:T(4,128)S(1)} %get-tuple-element.135), channel_id=1, source_target_pairs={{0,6},{1,7},{2,4},{3,5},{4,2},{5,3},{6,0},{7,1},{8,14},{9,15},{10,... | collective-permute-start | bytes 49160 | tf_op jit(solution)/shard_map/ppermute | solution.py:110
  47.6 1.5 collective-permute-done.8.refs_14_
  49.1 2.0 %collective-permute-done.9.refs_15_ = f32[4,1024]{1,0:T(4,128)S(1)} collective-permute-done((f32[4,1024]{1,0:T(4,128)S(1)}, f32[4,1024]{1,0:T(4,128)S(1)}, u32[]{:S(2)}, u32[]{:S(2)}) %collective-permute-start.9) | collective-permute-done | bytes 16416 | tf_op jit(solution)/shard_map/ppermute | solution.py:110
  51.1 9.3 %post.4 = (bf16[2,4,1024,256]{3,2,1,0:T(8,128)(2,1)S(1)}, bf16[2,4,1024,256]{3,2,1,0:T(8,128)(2,1)S(1)}, f32[2,4,48,128]{3,2,1,0:T(8,128)S(1)}, f32[4,512]{1,0:T...) custom-call(f32[2,4,256,1024]{3,2,1,0:T(8,128)S(1)} %get-tuple-elemen, ...), custom_call_target="tpu_custom_call" | custom-call | tf_op jit(solution)/shard_map/post/pallas_call | solution.py:595
  60.5 0.7 collective-permute-start.10
  61.2 3.5 %collective-permute-start.11 = (f32[4,512]{1,0:T(4,128)S(1)}, f32[4,512]{1,0:T(4,128)S(1)}, u32[]{:S(2)}, u32[]{:S(2)}) collective-permute-start(f32[4,512]{1,0:T(4,128)S(1)} %get-tuple-element.146), channel_id=1, source_target_pairs={{0,16},{8,24},{16,0},{24,8},{1,17},{9,25},{17,1},{25,9},{2,18},{10... | collective-permute-start | bytes 24584 | tf_op jit(solution)/shard_map/ppermute | solution.py:110
  64.9 9.8 %local.5 = (f32[2,4,256,1024]{3,2,1,0:T(8,128)S(1)}, f32[2,32,1024]{2,1,0:T(8,128)S(1)}, s32[512,1024]{1,0:T(8,128)S(1)}, s32[512,1024]{1,0:T(8,128)S(1)}) custom-call(bf16[2,4,1024,256]{3,2,1,0:T(8,128)(2,1)S(1)} %get-tuple-element.139.t_hi.refs_2_, bf16[2,4,1024,256]{3,2,1,0:T(8,128)(2,1)S(1)} %get-tuple-element.140.t_lo.refs_3_, ...), custom_call_target="tpu_custom_call" | custom-call | tf_op jit(solution)/shard_map/local/pallas_call | solution.py:516
  74.8 1.4 link.5
  76.3 0.6 collective-permute-start.14
  76.9 1.3 collective-permute-start.15
  78.7 1.2 collective-permute-start.17
  80.4 2.1 %collective-permute-start.19 = (f32[4,1024]{1,0:T(4,128)S(1)}, f32[4,1024]{1,0:T(4,128)S(1)}, u32[]{:S(2)}, u32[]{:S(2)}) collective-permute-start(f32[4,1024]{1,0:T(4,128)S(1)} %get-tuple-element.157), channel_id=1, source_target_pairs={{0,7},{1,6},{2,5},{3,4},{4,3},{5,2},{6,1},{7,0},{8,15},{9,14},{10,... | collective-permute-start | bytes 49160 | tf_op jit(solution)/shard_map/ppermute | solution.py:110
  82.6 2.1 %collective-permute-done.18.refs_14_ = f32[4,1024]{1,0:T(4,128)S(1)} collective-permute-done((f32[4,1024]{1,0:T(4,128)S(1)}, f32[4,1024]{1,0:T(4,128)S(1)}, u32[]{:S(2)}, u32[]{:S(2)}) %collective-permute-start.18) | collective-permute-done | bytes 16416 | tf_op jit(solution)/shard_map/ppermute | solution.py:110
  84.7 9.2 %post.5 = (bf16[2,4,1024,256]{3,2,1,0:T(8,128)(2,1)S(1)}, bf16[2,4,1024,256]{3,2,1,0:T(8,128)(2,1)S(1)}, f32[2,4,48,128]{3,2,1,0:T(8,128)S(1)}, f32[4,512]{1,0:T...) custom-call(f32[2,4,256,1024]{3,2,1,0:T(8,128)S(1)} %get-tuple-elemen, ...), custom_call_target="tpu_custom_call" | custom-call | tf_op jit(solution)/shard_map/post/pallas_call | solution.py:595
  94.3 3.8 %collective-permute-start.21 = (f32[4,512]{1,0:T(4,128)S(1)}, f32[4,512]{1,0:T(4,128)S(1)}, u32[]{:S(2)}, u32[]{:S(2)}) collective-permute-start(f32[4,512]{1,0:T(4,128)S(1)} %get-tuple-element.168), channel_id=1, source_target_pairs={{0,16},{8,24},{16,0},{24,8},{1,17},{9,25},{17,1},{25,9},{2,18},{10... | collective-permute-start | bytes 24584 | tf_op jit(solution)/shard_map/ppermute | solution.py:110
  98.3 9.9 %local.6 = (f32[2,4,256,1024]{3,2,1,0:T(8,128)S(1)}, f32[2,32,1024]{2,1,0:T(8,128)S(1)}, s32[512,1024]{1,0:T(8,128)S(1)}, s32[512,1024]{1,0:T(8,128)S(1)}, bf16[...) custom-call(bf16[2,4,1024,256]{3,2,1,0:T(8,128)(2,1)S(1)} %get-tuple-element.160.t_hi, ...), custom_call_target="tpu_custom_call" | custom-call | tf_op jit(solution)/shard_map/local/pallas_call | solution.py:516
  108.3 1.4 link.6
  109.8 1.3 collective-permute-start.24
  111.6 1.3 collective-permute-start.26
  113.3 2.2 %collective-permute-start.28 = (f32[4,1024]{1,0:T(4,128)S(1)}, f32[4,1024]{1,0:T(4,128)S(1)}, u32[]{:S(2)}, u32[]{:S(2)}) collective-permute-start(f32[4,1024]{1,0:T(4,128)S(1)} %get-tuple-element.178), channel_id=1, source_target_pairs={{0,6},{1,7},{2,4},{3,5},{4,2},{5,3},{6,0},{7,1},{8,14},{9,15},{10,... | collective-permute-start | bytes 49160 | tf_op jit(solution)/shard_map/ppermute | solution.py:110
  116.0 1.9 %collective-permute-done.28.refs_14_ = f32[4,1024]{1,0:T(4,128)S(1)} collective-permute-done((f32[4,1024]{1,0:T(4,128)S(1)}, f32[4,1024]{1,0:T(4,128)S(1)}, u32[]{:S(2)}, u32[]{:S(2)}) %collective-permute-start.28) | collective-permute-done | bytes 16416 | tf_op jit(solution)/shard_map/ppermute | solution.py:110
  118.0 1.6 %collective-permute-done.29.refs_15_ = f32[4,1024]{1,0:T(4,128)S(1)} collective-permute-done((f32[4,1024]{1,0:T(4,128)S(1)}, f32[4,1024]{1,0:T(4,128)S(1)}, u32[]{:S(2)}, u32[]{:S(2)}) %collective-permute-start.29) | collective-permute-done | bytes 16416 | tf_op jit(solution)/shard_map/ppermute | solution.py:110
  119.6 9.9 %post.6 = (bf16[2,4,1024,256]{3,2,1,0:T(8,128)(2,1)S(1)}, bf16[2,4,1024,256]{3,2,1,0:T(8,128)(2,1)S(1)}, f32[2,4,48,128]{3,2,1,0:T(8,128)S(1)}, f32[4,512]{1,0:T...) custom-call(f32[2,4,256,1024]{3,2,1,0:T(8,128)S(1)} %get-tuple-eleme, ...), custom_call_target="tpu_custom_call", output_to_operand_aliasing={{7}: (23, {})} | custom-call | tf_op jit(solution)/shard_map/post/pallas_call | solution.py:595
  129.9 3.8 %collective-permute-start.31 = (f32[4,512]{1,0:T(4,128)S(1)}, f32[4,512]{1,0:T(4,128)S(1)}, u32[]{:S(2)}, u32[]{:S(2)}) collective-permute-start(f32[4,512]{1,0:T(4,128)S(1)} %get-tuple-element.193), channel_id=1, source_target_pairs={{0,16},{8,24},{16,0},{24,8},{1,17},{9,25},{17,1},{25,9},{2,18},{10... | collective-permute-start | bytes 24584 | tf_op jit(solution)/shard_map/ppermute | solution.py:110
  133.9 9.9 %local.7 = (f32[2,4,256,1024]{3,2,1,0:T(8,128)S(1)}, f32[2,32,1024]{2,1,0:T(8,128)S(1)}, s32[512,1024]{1,0:T(8,128)S(1)}, f32[2,1,512,1024]{3,2,1,0:T(8,128)S(1)}) custom-call(bf16[2,4,1024,256]{3,2,1,0:T(8,128)(2,1)S(1)} %get-tuple-element.186.t_hi, bf16[2,4,1024,256]{3,2,1,0:T(8,128)(2,1)S(1)} %get-tuple-element.187.t_lo, ...), custom_call_target="tpu_custom_call" | custom-call | tf_op jit(solution)/shard_map/local/pallas_call | solution.py:516
  143.8 1.4 link.7
  145.3 0.6 collective-permute-start.34
  145.9 1.3 collective-permute-start.35
  147.7 1.2 collective-permute-start.37
  148.9 0.8 collective-permute-start.38
  149.7 1.9 %collective-permute-start.39 = (f32[4,1024]{1,0:T(4,128)S(1)}, f32[4,1024]{1,0:T(4,128)S(1)}, u32[]{:S(2)}, u32[]{:S(2)}) collective-permute-start(f32[4,1024]{1,0:T(4,128)S(1)} %get-tuple-element.204), channel_id=1, source_target_pairs={{0,7},{1,6},{2,5},{3,4},{4,3},{5,2},{6,1},{7,0},{8,15},{9,14},{10,... | collective-permute-start | bytes 49160 | tf_op jit(solution)/shard_map/ppermute | solution.py:110
  151.6 1.9 %collective-permute-done.38.refs_14_ = f32[4,1024]{1,0:T(4,128)S(1)} collective-permute-done((f32[4,1024]{1,0:T(4,128)S(1)}, f32[4,1024]{1,0:T(4,128)S(1)}, u32[]{:S(2)}, u32[]{:S(2)}) %collective-permute-start.38) | collective-permute-done | bytes 16416 | tf_op jit(solution)/shard_map/ppermute | solution.py:110
  153.7 6.4 %post.7 = (f32[2,1,512,1024]{3,2,1,0:T(8,128)}, f32[2,1,512,1024]{3,2,1,0:T(8,128)}, f32[4,512,1024]{2,1,0:T(8,128)}) custom-call(f32[2,4,256,1024]{3,2,1,0:T(8,128)S(1)} %get-tuple-element.189.refs_0_, f32[2,4,8,1024]{3,2,1,0:T(8,128)S(1)} %get-tuple-element.195.refs_1_, ...), custom_call_target="tpu_custom_call", output_to_operand_aliasing={{2}: (18, {})} | custom-call | tf_op jit(solution)/shard_map/post/pallas_call | solution.py:595
  (153 shorter events, 11.8 us)
Async XLA Ops:
  0.6 11.5 %copy-start.15 = (f32[512]{0:T(512)S(1)}, f32[512]{0:T(512)}, u32[]{:S(2)}) copy-start(f32[512]{0:T(512)} %constant.64) | copy-start | bytes 6148
  0.6 11.4 %copy-start.16 = (f32[512]{0:T(512)S(1)}, f32[512]{0:T(512)}, u32[]{:S(2)}) copy-start(f32[512]{0:T(512)} %constant.63) | copy-start | bytes 6148
  0.7 11.6 %copy-start.5 = (f32[1024]{0:T(1024)S(1)}, f32[1024]{0:T(1024)}, u32[]{:S(2)}) copy-start(f32[1024]{0:T(1024)} %constant.62) | copy-start | bytes 12292
  0.7 11.6 %copy-start.6 = (f32[1024]{0:T(1024)S(1)}, f32[1024]{0:T(1024)}, u32[]{:S(2)}) copy-start(f32[1024]{0:T(1024)} %constant.61) | copy-start | bytes 12292
  0.7 11.8 %copy-start.2 = (f32[10,512]{1,0:T(8,128)S(1)}, f32[10,512]{1,0:T(8,128)}, u32[]{:S(2)}) copy-start(f32[10,512]{1,0:T(8,128)} %constant.60) | copy-start | bytes 61444
  0.7 11.8 %copy-start.4 = (pred[10,512]{1,0:T(8,128)(4,1)S(1)}, pred[10,512]{1,0:T(8,128)(4,1)}, u32[]{:S(2)}) copy-start(pred[10,512]{1,0:T(8,128)(4,1)} %constant.54.clone) | copy-start | bytes 15364
  23.9 15.4 %collective-permute-start = (f32[4,512]{1,0:T(4,128)S(1)}, f32[4,512]{1,0:T(4,128)S(1)}, u32[]{:S(2)}, u32[]{:S(2)}) collective-permute-start(f32[4,512]{1,0:T(4,128)S(1)} %get-tuple-element.122), channel_id=1, source_target_pairs={{0,8},{8,0},{16,24},{24,16},{1,9},{9,1},{17,25},{25,17},{2,10},{10... | collective-permute-start | bytes 24584 | tf_op jit(solution)/shard_map/ppermute | solution.py:110
  27.0 12.3 %collective-permute-start.1 = (f32[4,512]{1,0:T(4,128)S(1)}, f32[4,512]{1,0:T(4,128)S(1)}, u32[]{:S(2)}, u32[]{:S(2)}) collective-permute-start(f32[4,512]{1,0:T(4,128)S(1)} %get-tuple-element.123), channel_id=1, source_target_pairs={{0,16},{8,24},{16,0},{24,8},{1,17},{9,25},{17,1},{25,9},{2,18},{10... | collective-permute-start | bytes 24584 | tf_op jit(solution)/shard_map/ppermute | solution.py:110
  29.6 9.7 %collective-permute-start.2 = (f32[4,512]{1,0:T(4,128)S(1)}, f32[4,512]{1,0:T(4,128)S(1)}, u32[]{:S(2)}, u32[]{:S(2)}) collective-permute-start(f32[4,512]{1,0:T(4,128)S(1)} %get-tuple-element.124), channel_id=1, source_target_pairs={{0,24},{8,16},{16,8},{24,0},{1,25},{9,17},{17,9},{25,1},{2,26},{10... | collective-permute-start | bytes 24584 | tf_op jit(solution)/shard_map/ppermute | solution.py:110
  40.7 3.7 %collective-permute-start.3 = (f32[4,1024]{1,0:T(4,128)S(1)}, f32[4,1024]{1,0:T(4,128)S(1)}, u32[]{:S(2)}, u32[]{:S(2)}) collective-permute-start(f32[4,1024]{1,0:T(4,128)S(1)} %get-tuple-element.130), channel_id=1, source_target_pairs={{0,1},{1,0},{2,3},{3,2},{4,5},{5,4},{6,7},{7,6},{8,9},{9,8},{10,11... | collective-permute-start | bytes 49160 | tf_op jit(solution)/shard_map/ppermute | solution.py:110
  40.8 6.2 %collective-permute-start.4 = (f32[4,1024]{1,0:T(4,128)S(1)}, f32[4,1024]{1,0:T(4,128)S(1)}, u32[]{:S(2)}, u32[]{:S(2)}) collective-permute-start(f32[4,1024]{1,0:T(4,128)S(1)} %get-tuple-element.131), channel_id=1, source_target_pairs={{0,2},{1,3},{2,0},{3,1},{4,6},{5,7},{6,4},{7,5},{8,10},{9,11},{10,... | collective-permute-start | bytes 49160 | tf_op jit(solution)/shard_map/ppermute | solution.py:110
  42.6 4.6 %collective-permute-start.5 = (f32[4,1024]{1,0:T(4,128)S(1)}, f32[4,1024]{1,0:T(4,128)S(1)}, u32[]{:S(2)}, u32[]{:S(2)}) collective-permute-start(f32[4,1024]{1,0:T(4,128)S(1)} %get-tuple-element.132), channel_id=1, source_target_pairs={{0,3},{1,2},{2,1},{3,0},{4,7},{5,6},{6,5},{7,4},{8,11},{9,10},{10,... | collective-permute-start | bytes 49160 | tf_op jit(solution)/shard_map/ppermute | solution.py:110
  42.7 4.5 %collective-permute-start.6 = (f32[4,1024]{1,0:T(4,128)S(1)}, f32[4,1024]{1,0:T(4,128)S(1)}, u32[]{:S(2)}, u32[]{:S(2)}) collective-permute-start(f32[4,1024]{1,0:T(4,128)S(1)} %get-tuple-element.133), channel_id=1, source_target_pairs={{0,4},{1,5},{2,6},{3,7},{4,0},{5,1},{6,2},{7,3},{8,12},{9,13},{10,... | collective-permute-start | bytes 49160 | tf_op jit(solution)/shard_map/ppermute | solution.py:110
  44.4 3.2 %collective-permute-start.7 = (f32[4,1024]{1,0:T(4,128)S(1)}, f32[4,1024]{1,0:T(4,128)S(1)}, u32[]{:S(2)}, u32[]{:S(2)}) collective-permute-start(f32[4,1024]{1,0:T(4,128)S(1)} %get-tuple-element.134), channel_id=1, source_target_pairs={{0,5},{1,4},{2,7},{3,6},{4,1},{5,0},{6,3},{7,2},{8,13},{9,12},{10,... | collective-permute-start | bytes 49160 | tf_op jit(solution)/shard_map/ppermute | solution.py:110
  44.4 4.7 %collective-permute-start.8 = (f32[4,1024]{1,0:T(4,128)S(1)}, f32[4,1024]{1,0:T(4,128)S(1)}, u32[]{:S(2)}, u32[]{:S(2)}) collective-permute-start(f32[4,1024]{1,0:T(4,128)S(1)} %get-tuple-element.135), channel_id=1, source_target_pairs={{0,6},{1,7},{2,4},{3,5},{4,2},{5,3},{6,0},{7,1},{8,14},{9,15},{10,... | collective-permute-start | bytes 49160 | tf_op jit(solution)/shard_map/ppermute | solution.py:110
  47.0 4.1 %collective-permute-start.9 = (f32[4,1024]{1,0:T(4,128)S(1)}, f32[4,1024]{1,0:T(4,128)S(1)}, u32[]{:S(2)}, u32[]{:S(2)}) collective-permute-start(f32[4,1024]{1,0:T(4,128)S(1)} %get-tuple-element.136), channel_id=1, source_target_pairs={{0,7},{1,6},{2,5},{3,4},{4,3},{5,2},{6,1},{7,0},{8,15},{9,14},{10,... | collective-permute-start | bytes 49160 | tf_op jit(solution)/shard_map/ppermute | solution.py:110
  60.4 14.3 %copy-start = (bf16[2,4,1024,256]{3,2,1,0:T(8,128)(2,1)}, bf16[2,4,1024,256]{3,2,1,0:T(8,128)(2,1)S(1)}, u32[]{:S(2)}) copy-start(bf16[2,4,1024,256]{3,2,1,0:T(8,128)(2,1)S(1)} %get-tuple-element.139.t_hi.refs_2_) | copy-start | bytes 12582916
  60.5 14.3 %copy-start.1 = (bf16[2,4,1024,256]{3,2,1,0:T(8,128)(2,1)}, bf16[2,4,1024,256]{3,2,1,0:T(8,128)(2,1)S(1)}, u32[]{:S(2)}) copy-start(bf16[2,4,1024,256]{3,2,1,0:T(8,128)(2,1)S(1)} %get-tuple-element.140.t_lo.refs_3_) | copy-start | bytes 12582916
  60.5 14.3 %collective-permute-start.10 = (f32[4,512]{1,0:T(4,128)S(1)}, f32[4,512]{1,0:T(4,128)S(1)}, u32[]{:S(2)}, u32[]{:S(2)}) collective-permute-start(f32[4,512]{1,0:T(4,128)S(1)} %get-tuple-element.145), channel_id=1, source_target_pairs={{0,8},{8,0},{16,24},{24,16},{1,9},{9,1},{17,25},{25,17},{2,10},{10... | collective-permute-start | bytes 24584 | tf_op jit(solution)/shard_map/ppermute | solution.py:110
  61.2 13.6 %collective-permute-start.11 = (f32[4,512]{1,0:T(4,128)S(1)}, f32[4,512]{1,0:T(4,128)S(1)}, u32[]{:S(2)}, u32[]{:S(2)}) collective-permute-start(f32[4,512]{1,0:T(4,128)S(1)} %get-tuple-element.146), channel_id=1, source_target_pairs={{0,16},{8,24},{16,0},{24,8},{1,17},{9,25},{17,1},{25,9},{2,18},{10... | collective-permute-start | bytes 24584 | tf_op jit(solution)/shard_map/ppermute | solution.py:110
  64.7 10.1 %collective-permute-start.12 = (f32[4,512]{1,0:T(4,128)S(1)}, f32[4,512]{1,0:T(4,128)S(1)}, u32[]{:S(2)}, u32[]{:S(2)}) collective-permute-start(f32[4,512]{1,0:T(4,128)S(1)} %get-tuple-element.147), channel_id=1, source_target_pairs={{0,24},{8,16},{16,8},{24,0},{1,25},{9,17},{17,9},{25,1},{2,26},{10... | collective-permute-start | bytes 24584 | tf_op jit(solution)/shard_map/ppermute | solution.py:110
  76.2 3.6 %collective-permute-start.13 = (f32[4,1024]{1,0:T(4,128)S(1)}, f32[4,1024]{1,0:T(4,128)S(1)}, u32[]{:S(2)}, u32[]{:S(2)}) collective-permute-start(f32[4,1024]{1,0:T(4,128)S(1)} %get-tuple-element.151), channel_id=1, source_target_pairs={{0,1},{1,0},{2,3},{3,2},{4,5},{5,4},{6,7},{7,6},{8,9},{9,8},{10,11... | collective-permute-start | bytes 49160 | tf_op jit(solution)/shard_map/ppermute | solution.py:110
  76.3 4.1 %collective-permute-start.14 = (f32[4,1024]{1,0:T(4,128)S(1)}, f32[4,1024]{1,0:T(4,128)S(1)}, u32[]{:S(2)}, u32[]{:S(2)}) collective-permute-start(f32[4,1024]{1,0:T(4,128)S(1)} %get-tuple-element.152), channel_id=1, source_target_pairs={{0,2},{1,3},{2,0},{3,1},{4,6},{5,7},{6,4},{7,5},{8,10},{9,11},{10,... | collective-permute-start | bytes 49160 | tf_op jit(solution)/shard_map/ppermute | solution.py:110
  76.9 5.7 %collective-permute-start.15 = (f32[4,1024]{1,0:T(4,128)S(1)}, f32[4,1024]{1,0:T(4,128)S(1)}, u32[]{:S(2)}, u32[]{:S(2)}) collective-permute-start(f32[4,1024]{1,0:T(4,128)S(1)} %get-tuple-element.153), channel_id=1, source_target_pairs={{0,3},{1,2},{2,1},{3,0},{4,7},{5,6},{6,5},{7,4},{8,11},{9,10},{10,... | collective-permute-start | bytes 49160 | tf_op jit(solution)/shard_map/ppermute | solution.py:110
  78.2 4.4 %collective-permute-start.16 = (f32[4,1024]{1,0:T(4,128)S(1)}, f32[4,1024]{1,0:T(4,128)S(1)}, u32[]{:S(2)}, u32[]{:S(2)}) collective-permute-start(f32[4,1024]{1,0:T(4,128)S(1)} %get-tuple-element.154), channel_id=1, source_target_pairs={{0,4},{1,5},{2,6},{3,7},{4,0},{5,1},{6,2},{7,3},{8,12},{9,13},{10,... | collective-permute-start | bytes 49160 | tf_op jit(solution)/shard_map/ppermute | solution.py:110
  78.7 3.9 %collective-permute-start.17 = (f32[4,1024]{1,0:T(4,128)S(1)}, f32[4,1024]{1,0:T(4,128)S(1)}, u32[]{:S(2)}, u32[]{:S(2)}) collective-permute-start(f32[4,1024]{1,0:T(4,128)S(1)} %get-tuple-element.155), channel_id=1, source_target_pairs={{0,5},{1,4},{2,7},{3,6},{4,1},{5,0},{6,3},{7,2},{8,13},{9,12},{10,... | collective-permute-start | bytes 49160 | tf_op jit(solution)/shard_map/ppermute | solution.py:110
  79.9 4.8 %collective-permute-start.18 = (f32[4,1024]{1,0:T(4,128)S(1)}, f32[4,1024]{1,0:T(4,128)S(1)}, u32[]{:S(2)}, u32[]{:S(2)}) collective-permute-start(f32[4,1024]{1,0:T(4,128)S(1)} %get-tuple-element.156), channel_id=1, source_target_pairs={{0,6},{1,7},{2,4},{3,5},{4,2},{5,3},{6,0},{7,1},{8,14},{9,15},{10,... | collective-permute-start | bytes 49160 | tf_op jit(solution)/shard_map/ppermute | solution.py:110
  80.4 4.2 %collective-permute-start.19 = (f32[4,1024]{1,0:T(4,128)S(1)}, f32[4,1024]{1,0:T(4,128)S(1)}, u32[]{:S(2)}, u32[]{:S(2)}) collective-permute-start(f32[4,1024]{1,0:T(4,128)S(1)} %get-tuple-element.157), channel_id=1, source_target_pairs={{0,7},{1,6},{2,5},{3,4},{4,3},{5,2},{6,1},{7,0},{8,15},{9,14},{10,... | collective-permute-start | bytes 49160 | tf_op jit(solution)/shard_map/ppermute | solution.py:110
  93.9 14.4 %collective-permute-start.20 = (f32[4,512]{1,0:T(4,128)S(1)}, f32[4,512]{1,0:T(4,128)S(1)}, u32[]{:S(2)}, u32[]{:S(2)}) collective-permute-start(f32[4,512]{1,0:T(4,128)S(1)} %get-tuple-element.167), channel_id=1, source_target_pairs={{0,8},{8,0},{16,24},{24,16},{1,9},{9,1},{17,25},{25,17},{2,10},{10... | collective-permute-start | bytes 24584 | tf_op jit(solution)/shard_map/ppermute | solution.py:110
  94.3 14.0 %collective-permute-start.21 = (f32[4,512]{1,0:T(4,128)S(1)}, f32[4,512]{1,0:T(4,128)S(1)}, u32[]{:S(2)}, u32[]{:S(2)}) collective-permute-start(f32[4,512]{1,0:T(4,128)S(1)} %get-tuple-element.168), channel_id=1, source_target_pairs={{0,16},{8,24},{16,0},{24,8},{1,17},{9,25},{17,1},{25,9},{2,18},{10... | collective-permute-start | bytes 24584 | tf_op jit(solution)/shard_map/ppermute | solution.py:110
  98.1 10.2 %collective-permute-start.22 = (f32[4,512]{1,0:T(4,128)S(1)}, f32[4,512]{1,0:T(4,128)S(1)}, u32[]{:S(2)}, u32[]{:S(2)}) collective-permute-start(f32[4,512]{1,0:T(4,128)S(1)} %get-tuple-element.169), channel_id=1, source_target_pairs={{0,24},{8,16},{16,8},{24,0},{1,25},{9,17},{17,9},{25,1},{2,26},{10... | collective-permute-start | bytes 24584 | tf_op jit(solution)/shard_map/ppermute | solution.py:110
  109.7 3.6 %collective-permute-start.23 = (f32[4,1024]{1,0:T(4,128)S(1)}, f32[4,1024]{1,0:T(4,128)S(1)}, u32[]{:S(2)}, u32[]{:S(2)}) collective-permute-start(f32[4,1024]{1,0:T(4,128)S(1)} %get-tuple-element.173), channel_id=1, source_target_pairs={{0,1},{1,0},{2,3},{3,2},{4,5},{5,4},{6,7},{7,6},{8,9},{9,8},{10,11... | collective-permute-start | bytes 49160 | tf_op jit(solution)/shard_map/ppermute | solution.py:110
  109.8 5.7 %collective-permute-start.24 = (f32[4,1024]{1,0:T(4,128)S(1)}, f32[4,1024]{1,0:T(4,128)S(1)}, u32[]{:S(2)}, u32[]{:S(2)}) collective-permute-start(f32[4,1024]{1,0:T(4,128)S(1)} %get-tuple-element.174), channel_id=1, source_target_pairs={{0,2},{1,3},{2,0},{3,1},{4,6},{5,7},{6,4},{7,5},{8,10},{9,11},{10,... | collective-permute-start | bytes 49160 | tf_op jit(solution)/shard_map/ppermute | solution.py:110
  111.1 5.0 %collective-permute-start.25 = (f32[4,1024]{1,0:T(4,128)S(1)}, f32[4,1024]{1,0:T(4,128)S(1)}, u32[]{:S(2)}, u32[]{:S(2)}) collective-permute-start(f32[4,1024]{1,0:T(4,128)S(1)} %get-tuple-element.175), channel_id=1, source_target_pairs={{0,3},{1,2},{2,1},{3,0},{4,7},{5,6},{6,5},{7,4},{8,11},{9,10},{10,... | collective-permute-start | bytes 49160 | tf_op jit(solution)/shard_map/ppermute | solution.py:110
  111.6 4.4 %collective-permute-start.26 = (f32[4,1024]{1,0:T(4,128)S(1)}, f32[4,1024]{1,0:T(4,128)S(1)}, u32[]{:S(2)}, u32[]{:S(2)}) collective-permute-start(f32[4,1024]{1,0:T(4,128)S(1)} %get-tuple-element.176), channel_id=1, source_target_pairs={{0,4},{1,5},{2,6},{3,7},{4,0},{5,1},{6,2},{7,3},{8,12},{9,13},{10,... | collective-permute-start | bytes 49160 | tf_op jit(solution)/shard_map/ppermute | solution.py:110
  112.9 3.2 %collective-permute-start.27 = (f32[4,1024]{1,0:T(4,128)S(1)}, f32[4,1024]{1,0:T(4,128)S(1)}, u32[]{:S(2)}, u32[]{:S(2)}) collective-permute-start(f32[4,1024]{1,0:T(4,128)S(1)} %get-tuple-element.177), channel_id=1, source_target_pairs={{0,5},{1,4},{2,7},{3,6},{4,1},{5,0},{6,3},{7,2},{8,13},{9,12},{10,... | collective-permute-start | bytes 49160 | tf_op jit(solution)/shard_map/ppermute | solution.py:110
  113.3 4.6 %collective-permute-start.28 = (f32[4,1024]{1,0:T(4,128)S(1)}, f32[4,1024]{1,0:T(4,128)S(1)}, u32[]{:S(2)}, u32[]{:S(2)}) collective-permute-start(f32[4,1024]{1,0:T(4,128)S(1)} %get-tuple-element.178), channel_id=1, source_target_pairs={{0,6},{1,7},{2,4},{3,5},{4,2},{5,3},{6,0},{7,1},{8,14},{9,15},{10,... | collective-permute-start | bytes 49160 | tf_op jit(solution)/shard_map/ppermute | solution.py:110
  115.5 4.1 %collective-permute-start.29 = (f32[4,1024]{1,0:T(4,128)S(1)}, f32[4,1024]{1,0:T(4,128)S(1)}, u32[]{:S(2)}, u32[]{:S(2)}) collective-permute-start(f32[4,1024]{1,0:T(4,128)S(1)} %get-tuple-element.179), channel_id=1, source_target_pairs={{0,7},{1,6},{2,5},{3,4},{4,3},{5,2},{6,1},{7,0},{8,15},{9,14},{10,... | collective-permute-start | bytes 49160 | tf_op jit(solution)/shard_map/ppermute | solution.py:110
  129.4 14.4 %collective-permute-start.30 = (f32[4,512]{1,0:T(4,128)S(1)}, f32[4,512]{1,0:T(4,128)S(1)}, u32[]{:S(2)}, u32[]{:S(2)}) collective-permute-start(f32[4,512]{1,0:T(4,128)S(1)} %get-tuple-element.192), channel_id=1, source_target_pairs={{0,8},{8,0},{16,24},{24,16},{1,9},{9,1},{17,25},{25,17},{2,10},{10... | collective-permute-start | bytes 24584 | tf_op jit(solution)/shard_map/ppermute | solution.py:110
  129.9 14.0 %collective-permute-start.31 = (f32[4,512]{1,0:T(4,128)S(1)}, f32[4,512]{1,0:T(4,128)S(1)}, u32[]{:S(2)}, u32[]{:S(2)}) collective-permute-start(f32[4,512]{1,0:T(4,128)S(1)} %get-tuple-element.193), channel_id=1, source_target_pairs={{0,16},{8,24},{16,0},{24,8},{1,17},{9,25},{17,1},{25,9},{2,18},{10... | collective-permute-start | bytes 24584 | tf_op jit(solution)/shard_map/ppermute | solution.py:110
  133.7 10.2 %collective-permute-start.32 = (f32[4,512]{1,0:T(4,128)S(1)}, f32[4,512]{1,0:T(4,128)S(1)}, u32[]{:S(2)}, u32[]{:S(2)}) collective-permute-start(f32[4,512]{1,0:T(4,128)S(1)} %get-tuple-element.194), channel_id=1, source_target_pairs={{0,24},{8,16},{16,8},{24,0},{1,25},{9,17},{17,9},{25,1},{2,26},{10... | collective-permute-start | bytes 24584 | tf_op jit(solution)/shard_map/ppermute | solution.py:110
  145.3 3.6 %collective-permute-start.33 = (f32[4,1024]{1,0:T(4,128)S(1)}, f32[4,1024]{1,0:T(4,128)S(1)}, u32[]{:S(2)}, u32[]{:S(2)}) collective-permute-start(f32[4,1024]{1,0:T(4,128)S(1)} %get-tuple-element.198), channel_id=1, source_target_pairs={{0,1},{1,0},{2,3},{3,2},{4,5},{5,4},{6,7},{7,6},{8,9},{9,8},{10,11... | collective-permute-start | bytes 49160 | tf_op jit(solution)/shard_map/ppermute | solution.py:110
  145.3 4.3 %collective-permute-start.34 = (f32[4,1024]{1,0:T(4,128)S(1)}, f32[4,1024]{1,0:T(4,128)S(1)}, u32[]{:S(2)}, u32[]{:S(2)}) collective-permute-start(f32[4,1024]{1,0:T(4,128)S(1)} %get-tuple-element.199), channel_id=1, source_target_pairs={{0,2},{1,3},{2,0},{3,1},{4,6},{5,7},{6,4},{7,5},{8,10},{9,11},{10,... | collective-permute-start | bytes 49160 | tf_op jit(solution)/shard_map/ppermute | solution.py:110
  145.9 5.7 %collective-permute-start.35 = (f32[4,1024]{1,0:T(4,128)S(1)}, f32[4,1024]{1,0:T(4,128)S(1)}, u32[]{:S(2)}, u32[]{:S(2)}) collective-permute-start(f32[4,1024]{1,0:T(4,128)S(1)} %get-tuple-element.200), channel_id=1, source_target_pairs={{0,3},{1,2},{2,1},{3,0},{4,7},{5,6},{6,5},{7,4},{8,11},{9,10},{10,... | collective-permute-start | bytes 49160 | tf_op jit(solution)/shard_map/ppermute | solution.py:110
  147.2 4.4 %collective-permute-start.36 = (f32[4,1024]{1,0:T(4,128)S(1)}, f32[4,1024]{1,0:T(4,128)S(1)}, u32[]{:S(2)}, u32[]{:S(2)}) collective-permute-start(f32[4,1024]{1,0:T(4,128)S(1)} %get-tuple-element.201), channel_id=1, source_target_pairs={{0,4},{1,5},{2,6},{3,7},{4,0},{5,1},{6,2},{7,3},{8,12},{9,13},{10,... | collective-permute-start | bytes 49160 | tf_op jit(solution)/shard_map/ppermute | solution.py:110
  147.7 3.9 %collective-permute-start.37 = (f32[4,1024]{1,0:T(4,128)S(1)}, f32[4,1024]{1,0:T(4,128)S(1)}, u32[]{:S(2)}, u32[]{:S(2)}) collective-permute-start(f32[4,1024]{1,0:T(4,128)S(1)} %get-tuple-element.202), channel_id=1, source_target_pairs={{0,5},{1,4},{2,7},{3,6},{4,1},{5,0},{6,3},{7,2},{8,13},{9,12},{10,... | collective-permute-start | bytes 49160 | tf_op jit(solution)/shard_map/ppermute | solution.py:110
  148.9 4.6 %collective-permute-start.38 = (f32[4,1024]{1,0:T(4,128)S(1)}, f32[4,1024]{1,0:T(4,128)S(1)}, u32[]{:S(2)}, u32[]{:S(2)}) collective-permute-start(f32[4,1024]{1,0:T(4,128)S(1)} %get-tuple-element.203), channel_id=1, source_target_pairs={{0,6},{1,7},{2,4},{3,5},{4,2},{5,3},{6,0},{7,1},{8,14},{9,15},{10,... | collective-permute-start | bytes 49160 | tf_op jit(solution)/shard_map/ppermute | solution.py:110
  149.7 4.1 %collective-permute-start.39 = (f32[4,1024]{1,0:T(4,128)S(1)}, f32[4,1024]{1,0:T(4,128)S(1)}, u32[]{:S(2)}, u32[]{:S(2)}) collective-permute-start(f32[4,1024]{1,0:T(4,128)S(1)} %get-tuple-element.204), channel_id=1, source_target_pairs={{0,7},{1,6},{2,5},{3,4},{4,3},{5,2},{6,1},{7,0},{8,15},{9,14},{10,... | collective-permute-start | bytes 49160 | tf_op jit(solution)/shard_map/ppermute | solution.py:110
  (14 other events, 16.5 us)
where the time goes:
time: 163 us; the launch traced here: 160 us
  Pallas kernels  87.1 us (53%)
  starting transfers between devices  44.4 us (27%)
  waiting for transfers between devices  11.8 us (7%)
  other arithmetic  10.5 us (6%)
  between operations  4.21 us (3%)
  local copies, waits for them, and re-layouts  2.47 us (2%)
    ppermute x40, starting transfers between devices, exchange(): got.append(lax.ppermute(pieces[s], axis, pairs))  44.4 us
    pallas_call x4, Pallas kernels, local(): pl.pallas_call(functools.partial(local_kernel, nbx, nby, tuple((level for...  39.3 us
    pallas_call x4, Pallas kernels, on_device(): pl.pallas_call(functools.partial(post_kernel, plan, nbx, nby, county, cou...  34.7 us
    ppermute x40, waiting for transfers between devices, exchange(): got.append(lax.ppermute(pieces[s], axis, pairs))  11.8 us
    pallas_call x1, Pallas kernels, on_device(): pl.pallas_call(functools.partial(first_kernel, nby, county), grid=(nbx,),...  7.4 us
    another operation x12, other arithmetic, link_coefs(): return jnp.stack([*send_f, *send_b, *recv_f, *recv_b])  5.83 us
    pallas_call x4, Pallas kernels, on_device(): link(x_local, coef_y, coef_x, sx3, edge_y, my3, *recv_y)  5.62 us
  transfers between devices with their start and end apart: 40, of which 8 were waited for; matrix products, arithmetic and copies ran while one was open for 0% of the time, Pallas kernels for 25%

commit v1 on v0

--- a/solution.py
+++ b/solution.py
@@ -113,27 +113,18 @@
 
 def link_coefs(modulus, angle, off, end, count, mine, length):
     slots = np.arange(count, dtype=np.int32)
-    root = (modulus * jnp.cos(angle), modulus * jnp.sin(angle))
-    one = jnp.ones((count,), F32)
-    zero = jnp.zeros((count,), F32)
-
-    def factors(other):
-        far = root_powers(modulus, angle, length * (2 * count - 2 - mine - other))
-        near = root_powers(modulus, angle, length * jnp.maximum(jnp.abs(other - mine) - 1, 0))
-        return near, complex_mul(end, far)
-
-    other = partner(mine, slots, count, 1)
-    near, tail = factors(other)
-    head = complex_mul(complex_mul(off, root), near)
-    before = other < mine
-    send_f = (jnp.where(before, tail[0], one), jnp.where(before, tail[1], zero))
-    send_b = (jnp.where(before, head[0], zero), jnp.where(before, head[1], zero))
-    other = partner(mine, slots, count, -1)
-    near, tail = factors(other)
-    before, after = other < mine, other > mine
-    recv_f = (jnp.where(before, near[0], zero), jnp.where(before, near[1], zero))
-    recv_b = (jnp.where(after, one, tail[0]), jnp.where(after, zero, tail[1]))
-    return jnp.stack([*send_f, *send_b, *recv_f, *recv_b])
+    row = np.arange(8)[:, None]
+    other = jnp.where(row < 4, partner(mine, slots, count, 1)[None], partner(mine, slots, count, -1)[None])
+    far = (row < 2) | (row >= 6)
+    apart = jnp.where(far, 2 * count - 2 - mine - other, jnp.maximum(jnp.abs(other - mine) - 1, 0))
+    power = root_powers(modulus, angle, length * apart)
+    head = complex_mul(off, (modulus * jnp.cos(angle), modulus * jnp.sin(angle)))
+    lead = (row == 2) | (row == 3)
+    factor = [jnp.where(far, end[n], jnp.where(lead, head[n], 1.0 - n)) for n in range(2)]
+    value = complex_mul(factor, power)
+    real = row % 2 == 0
+    used = jnp.where(row < 6, other < mine, other <= mine)
+    return jnp.where(used, jnp.where(real, value[0], value[1]), jnp.where(far & real, 1.0, 0.0))
 
 
 def split3(x, first):

time: 163 us -> 156 us (0.957)
  other arithmetic: 10.5 us -> 4.11 us
    another operation x12 -> x0, other arithmetic: 5.83 us -> none  [link_coefs(): return jnp.stack([*send_f, *send_b, *recv_f, *recv_b])]
where the time goes in v1:
time: 156 us; the launch traced here: 153 us
  Pallas kernels  86.3 us (55%)
  starting transfers between devices  44.4 us (28%)
  waiting for transfers between devices  11.8 us (8%)
  between operations  4.17 us (3%)
  other arithmetic  4.11 us (3%)
  local copies, waits for them, and re-layouts  2.55 us (2%)
    ppermute x40, starting transfers between devices, exchange(): got.append(lax.ppermute(pieces[s], axis, pairs))  44.4 us
    pallas_call x4, Pallas kernels, local(): pl.pallas_call(functools.partial(local_kernel, nbx, nby, tuple((level for...  39 us
    pallas_call x4, Pallas kernels, on_device(): pl.pallas_call(functools.partial(post_kernel, plan, nbx, nby, county, cou...  34.3 us
    ppermute x40, waiting for transfers between devices, exchange(): got.append(lax.ppermute(pieces[s], axis, pairs))  11.8 us
    pallas_call x1, Pallas kernels, on_device(): pl.pallas_call(functools.partial(first_kernel, nby, county), grid=(nbx,),...  7.38 us
    pallas_call x4, Pallas kernels, on_device(): link(x_local, coef_y, coef_x, sx3, edge_y, my3, *recv_y)  5.63 us
  transfers between devices with their start and end apart: 40, of which 8 were waited for; matrix products, arithmetic and copies ran while one was open for 0% of the time, Pallas kernels for 25%

profile of v1, /device:TPU:0, one launch (start us, length us, event | category | flops | bytes accessed | tf_op | source)
XLA Modules:
  0.0 153.3 jit_solution(9941192062885579823)
XLA Ops:
  2.4 0.7 fusion.60
  3.2 1.3 multiply_select_fusion
  7.4 1.3 copy.48
  10.2 7.4 %first.1 = (bf16[2,4,1024,256]{3,2,1,0:T(8,128)(2,1)S(1)}, bf16[2,4,1024,256]{3,2,1,0:T(8,128)(2,1)S(1)}, f32[2,4,48,128]{3,2,1,0:T(8,128)S(1)}, f32[4,512]{1,0:...) custom-call(f32[2,1,512,1024]{3,2,1,0:T(8,128)} %refs_1_.7, ...), custom_call_target="tpu_custom_call" | custom-call | tf_op jit(solution)/shard_map/first/pallas_call | solution.py:495
  17.6 3.1 %collective-permute-start = (f32[4,512]{1,0:T(4,128)S(1)}, f32[4,512]{1,0:T(4,128)S(1)}, u32[]{:S(2)}, u32[]{:S(2)}) collective-permute-start(f32[4,512]{1,0:T(4,128)S(1)} %get-tuple-element.122), channel_id=1, source_target_pairs={{0,8},{8,0},{16,24},{24,16},{1,9},{9,1},{17,25},{25,17},{2,10},{10... | collective-permute-start | bytes 24584 | tf_op jit(solution)/shard_map/ppermute | solution.py:110
  20.7 2.6 %collective-permute-start.1 = (f32[4,512]{1,0:T(4,128)S(1)}, f32[4,512]{1,0:T(4,128)S(1)}, u32[]{:S(2)}, u32[]{:S(2)}) collective-permute-start(f32[4,512]{1,0:T(4,128)S(1)} %get-tuple-element.123), channel_id=1, source_target_pairs={{0,16},{8,24},{16,0},{24,8},{1,17},{9,25},{17,1},{25,9},{2,18},{10... | collective-permute-start | bytes 24584 | tf_op jit(solution)/shard_map/ppermute | solution.py:110
  23.3 9.6 %local.4 = (f32[2,4,256,1024]{3,2,1,0:T(8,128)S(1)}, f32[2,32,1024]{2,1,0:T(8,128)S(1)}, s32[512,1024]{1,0:T(8,128)S(1)}, s32[512,1024]{1,0:T(8,128)S(1)}) custom-call(bf16[2,4,1024,256]{3,2,1,0:T(8,128)(2,1)S(1)} %get-tuple-element.111.t_hi, bf16[2,4,1024,256]{3,2,1,0:T(8,128)(2,1)S(1)} %get-tuple-element.112.t_lo, ...), custom_call_target="tpu_custom_call" | custom-call | tf_op jit(solution)/shard_map/local/pallas_call | solution.py:507
  33.0 1.4 link.4
  34.4 1.8 %collective-permute-start.4 = (f32[4,1024]{1,0:T(4,128)S(1)}, f32[4,1024]{1,0:T(4,128)S(1)}, u32[]{:S(2)}, u32[]{:S(2)}) collective-permute-start(f32[4,1024]{1,0:T(4,128)S(1)} %get-tuple-element.131), channel_id=1, source_target_pairs={{0,2},{1,3},{2,0},{3,1},{4,6},{5,7},{6,4},{7,5},{8,10},{9,11},{10,... | collective-permute-start | bytes 49160 | tf_op jit(solution)/shard_map/ppermute | solution.py:110
  36.3 1.8 %collective-permute-start.6 = (f32[4,1024]{1,0:T(4,128)S(1)}, f32[4,1024]{1,0:T(4,128)S(1)}, u32[]{:S(2)}, u32[]{:S(2)}) collective-permute-start(f32[4,1024]{1,0:T(4,128)S(1)} %get-tuple-element.133), channel_id=1, source_target_pairs={{0,4},{1,5},{2,6},{3,7},{4,0},{5,1},{6,2},{7,3},{8,12},{9,13},{10,... | collective-permute-start | bytes 49160 | tf_op jit(solution)/shard_map/ppermute | solution.py:110
  38.1 2.6 %collective-permute-start.8 = (f32[4,1024]{1,0:T(4,128)S(1)}, f32[4,1024]{1,0:T(4,128)S(1)}, u32[]{:S(2)}, u32[]{:S(2)}) collective-permute-start(f32[4,1024]{1,0:T(4,128)S(1)} %get-tuple-element.135), channel_id=1, source_target_pairs={{0,6},{1,7},{2,4},{3,5},{4,2},{5,3},{6,0},{7,1},{8,14},{9,15},{10,... | collective-permute-start | bytes 49160 | tf_op jit(solution)/shard_map/ppermute | solution.py:110
  41.2 1.5 collective-permute-done.8.refs_14_
  42.7 2.0 %collective-permute-done.9.refs_15_ = f32[4,1024]{1,0:T(4,128)S(1)} collective-permute-done((f32[4,1024]{1,0:T(4,128)S(1)}, f32[4,1024]{1,0:T(4,128)S(1)}, u32[]{:S(2)}, u32[]{:S(2)}) %collective-permute-start.9) | collective-permute-done | bytes 16416 | tf_op jit(solution)/shard_map/ppermute | solution.py:110
  44.8 9.2 %post.4 = (bf16[2,4,1024,256]{3,2,1,0:T(8,128)(2,1)S(1)}, bf16[2,4,1024,256]{3,2,1,0:T(8,128)(2,1)S(1)}, f32[2,4,48,128]{3,2,1,0:T(8,128)S(1)}, f32[4,512]{1,0:T...) custom-call(f32[2,4,256,1024]{3,2,1,0:T(8,128)S(1)} %get-tuple-elemen, ...), custom_call_target="tpu_custom_call" | custom-call | tf_op jit(solution)/shard_map/post/pallas_call | solution.py:586
  54.0 0.7 collective-permute-start.10
  54.7 3.5 %collective-permute-start.11 = (f32[4,512]{1,0:T(4,128)S(1)}, f32[4,512]{1,0:T(4,128)S(1)}, u32[]{:S(2)}, u32[]{:S(2)}) collective-permute-start(f32[4,512]{1,0:T(4,128)S(1)} %get-tuple-element.146), channel_id=1, source_target_pairs={{0,16},{8,24},{16,0},{24,8},{1,17},{9,25},{17,1},{25,9},{2,18},{10... | collective-permute-start | bytes 24584 | tf_op jit(solution)/shard_map/ppermute | solution.py:110
  58.4 9.7 %local.5 = (f32[2,4,256,1024]{3,2,1,0:T(8,128)S(1)}, f32[2,32,1024]{2,1,0:T(8,128)S(1)}, s32[512,1024]{1,0:T(8,128)S(1)}, s32[512,1024]{1,0:T(8,128)S(1)}) custom-call(bf16[2,4,1024,256]{3,2,1,0:T(8,128)(2,1)S(1)} %get-tuple-element.139.t_hi.refs_2_, bf16[2,4,1024,256]{3,2,1,0:T(8,128)(2,1)S(1)} %get-tuple-element.140.t_lo.refs_3_, ...), custom_call_target="tpu_custom_call" | custom-call | tf_op jit(solution)/shard_map/local/pallas_call | solution.py:507
  68.3 1.4 link.5
  69.7 0.6 collective-permute-start.14
  70.3 1.3 collective-permute-start.15
  71.6 0.5 collective-permute-start.16
  72.1 1.2 collective-permute-start.17
  73.3 0.6 collective-permute-start.18
  73.9 2.1 %collective-permute-start.19 = (f32[4,1024]{1,0:T(4,128)S(1)}, f32[4,1024]{1,0:T(4,128)S(1)}, u32[]{:S(2)}, u32[]{:S(2)}) collective-permute-start(f32[4,1024]{1,0:T(4,128)S(1)} %get-tuple-element.157), channel_id=1, source_target_pairs={{0,7},{1,6},{2,5},{3,4},{4,3},{5,2},{6,1},{7,0},{8,15},{9,14},{10,... | collective-permute-start | bytes 49160 | tf_op jit(solution)/shard_map/ppermute | solution.py:110
  76.0 2.1 %collective-permute-done.18.refs_14_ = f32[4,1024]{1,0:T(4,128)S(1)} collective-permute-done((f32[4,1024]{1,0:T(4,128)S(1)}, f32[4,1024]{1,0:T(4,128)S(1)}, u32[]{:S(2)}, u32[]{:S(2)}) %collective-permute-start.18) | collective-permute-done | bytes 16416 | tf_op jit(solution)/shard_map/ppermute | solution.py:110
  78.1 9.0 %post.5 = (bf16[2,4,1024,256]{3,2,1,0:T(8,128)(2,1)S(1)}, bf16[2,4,1024,256]{3,2,1,0:T(8,128)(2,1)S(1)}, f32[2,4,48,128]{3,2,1,0:T(8,128)S(1)}, f32[4,512]{1,0:T...) custom-call(f32[2,4,256,1024]{3,2,1,0:T(8,128)S(1)} %get-tuple-elemen, ...), custom_call_target="tpu_custom_call" | custom-call | tf_op jit(solution)/shard_map/post/pallas_call | solution.py:586
  87.6 3.8 %collective-permute-start.21 = (f32[4,512]{1,0:T(4,128)S(1)}, f32[4,512]{1,0:T(4,128)S(1)}, u32[]{:S(2)}, u32[]{:S(2)}) collective-permute-start(f32[4,512]{1,0:T(4,128)S(1)} %get-tuple-element.168), channel_id=1, source_target_pairs={{0,16},{8,24},{16,0},{24,8},{1,17},{9,25},{17,1},{25,9},{2,18},{10... | collective-permute-start | bytes 24584 | tf_op jit(solution)/shard_map/ppermute | solution.py:110
  91.6 9.8 %local.6 = (f32[2,4,256,1024]{3,2,1,0:T(8,128)S(1)}, f32[2,32,1024]{2,1,0:T(8,128)S(1)}, s32[512,1024]{1,0:T(8,128)S(1)}, s32[512,1024]{1,0:T(8,128)S(1)}, bf16[...) custom-call(bf16[2,4,1024,256]{3,2,1,0:T(8,128)(2,1)S(1)} %get-tuple-element.160.t_hi, ...), custom_call_target="tpu_custom_call" | custom-call | tf_op jit(solution)/shard_map/local/pallas_call | solution.py:507
  101.5 1.4 link.6
  103.0 1.3 collective-permute-start.24
  104.2 0.6 collective-permute-start.25
  104.8 1.3 collective-permute-start.26
  106.5 2.2 %collective-permute-start.28 = (f32[4,1024]{1,0:T(4,128)S(1)}, f32[4,1024]{1,0:T(4,128)S(1)}, u32[]{:S(2)}, u32[]{:S(2)}) collective-permute-start(f32[4,1024]{1,0:T(4,128)S(1)} %get-tuple-element.178), channel_id=1, source_target_pairs={{0,6},{1,7},{2,4},{3,5},{4,2},{5,3},{6,0},{7,1},{8,14},{9,15},{10,... | collective-permute-start | bytes 49160 | tf_op jit(solution)/shard_map/ppermute | solution.py:110
  108.7 0.5 collective-permute-start.29
  109.2 1.9 %collective-permute-done.28.refs_14_ = f32[4,1024]{1,0:T(4,128)S(1)} collective-permute-done((f32[4,1024]{1,0:T(4,128)S(1)}, f32[4,1024]{1,0:T(4,128)S(1)}, u32[]{:S(2)}, u32[]{:S(2)}) %collective-permute-start.28) | collective-permute-done | bytes 16416 | tf_op jit(solution)/shard_map/ppermute | solution.py:110
  111.2 1.6 %collective-permute-done.29.refs_15_ = f32[4,1024]{1,0:T(4,128)S(1)} collective-permute-done((f32[4,1024]{1,0:T(4,128)S(1)}, f32[4,1024]{1,0:T(4,128)S(1)}, u32[]{:S(2)}, u32[]{:S(2)}) %collective-permute-start.29) | collective-permute-done | bytes 16416 | tf_op jit(solution)/shard_map/ppermute | solution.py:110
  112.8 9.7 %post.6 = (bf16[2,4,1024,256]{3,2,1,0:T(8,128)(2,1)S(1)}, bf16[2,4,1024,256]{3,2,1,0:T(8,128)(2,1)S(1)}, f32[2,4,48,128]{3,2,1,0:T(8,128)S(1)}, f32[4,512]{1,0:T...) custom-call(f32[2,4,256,1024]{3,2,1,0:T(8,128)S(1)} %get-tuple-eleme, ...), custom_call_target="tpu_custom_call", output_to_operand_aliasing={{7}: (23, {})} | custom-call | tf_op jit(solution)/shard_map/post/pallas_call | solution.py:586
  122.9 3.8 %collective-permute-start.31 = (f32[4,512]{1,0:T(4,128)S(1)}, f32[4,512]{1,0:T(4,128)S(1)}, u32[]{:S(2)}, u32[]{:S(2)}) collective-permute-start(f32[4,512]{1,0:T(4,128)S(1)} %get-tuple-element.193), channel_id=1, source_target_pairs={{0,16},{8,24},{16,0},{24,8},{1,17},{9,25},{17,1},{25,9},{2,18},{10... | collective-permute-start | bytes 24584 | tf_op jit(solution)/shard_map/ppermute | solution.py:110
  126.9 9.8 %local.7 = (f32[2,4,256,1024]{3,2,1,0:T(8,128)S(1)}, f32[2,32,1024]{2,1,0:T(8,128)S(1)}, s32[512,1024]{1,0:T(8,128)S(1)}, f32[2,1,512,1024]{3,2,1,0:T(8,128)S(1)}) custom-call(bf16[2,4,1024,256]{3,2,1,0:T(8,128)(2,1)S(1)} %get-tuple-element.186.t_hi, bf16[2,4,1024,256]{3,2,1,0:T(8,128)(2,1)S(1)} %get-tuple-element.187.t_lo, ...), custom_call_target="tpu_custom_call" | custom-call | tf_op jit(solution)/shard_map/local/pallas_call | solution.py:507
  136.8 1.4 link.7
  138.3 0.6 collective-permute-start.34
  138.9 1.3 collective-permute-start.35
  140.2 0.5 collective-permute-start.36
  140.7 1.2 collective-permute-start.37
  141.9 0.8 collective-permute-start.38
  142.6 1.9 %collective-permute-start.39 = (f32[4,1024]{1,0:T(4,128)S(1)}, f32[4,1024]{1,0:T(4,128)S(1)}, u32[]{:S(2)}, u32[]{:S(2)}) collective-permute-start(f32[4,1024]{1,0:T(4,128)S(1)} %get-tuple-element.204), channel_id=1, source_target_pairs={{0,7},{1,6},{2,5},{3,4},{4,3},{5,2},{6,1},{7,0},{8,15},{9,14},{10,... | collective-permute-start | bytes 49160 | tf_op jit(solution)/shard_map/ppermute | solution.py:110
  144.6 1.9 %collective-permute-done.38.refs_14_ = f32[4,1024]{1,0:T(4,128)S(1)} collective-permute-done((f32[4,1024]{1,0:T(4,128)S(1)}, f32[4,1024]{1,0:T(4,128)S(1)}, u32[]{:S(2)}, u32[]{:S(2)}) %collective-permute-start.38) | collective-permute-done | bytes 16416 | tf_op jit(solution)/shard_map/ppermute | solution.py:110
  146.7 6.4 %post.7 = (f32[2,1,512,1024]{3,2,1,0:T(8,128)}, f32[2,1,512,1024]{3,2,1,0:T(8,128)}, f32[4,512,1024]{2,1,0:T(8,128)}) custom-call(f32[2,4,256,1024]{3,2,1,0:T(8,128)S(1)} %get-tuple-element.189.refs_0_, f32[2,4,8,1024]{3,2,1,0:T(8,128)S(1)} %get-tuple-element.195.refs_1_, ...), custom_call_target="tpu_custom_call", output_to_operand_aliasing={{2}: (18, {})} | custom-call | tf_op jit(solution)/shard_map/post/pallas_call | solution.py:586
  (136 shorter events, 6.4 us)
Async XLA Ops:
  0.6 5.7 %copy-start.8 = (f32[512]{0:T(512)S(1)}, f32[512]{0:T(512)}, u32[]{:S(2)}) copy-start(f32[512]{0:T(512)} %constant.147) | copy-start | bytes 6148
  0.6 5.7 %copy-start.9 = (f32[512]{0:T(512)S(1)}, f32[512]{0:T(512)}, u32[]{:S(2)}) copy-start(f32[512]{0:T(512)} %constant.146) | copy-start | bytes 6148
  0.7 5.9 %copy-start.6 = (f32[1024]{0:T(1024)S(1)}, f32[1024]{0:T(1024)}, u32[]{:S(2)}) copy-start(f32[1024]{0:T(1024)} %constant.145) | copy-start | bytes 12292
  0.7 5.9 %copy-start.7 = (f32[1024]{0:T(1024)S(1)}, f32[1024]{0:T(1024)}, u32[]{:S(2)}) copy-start(f32[1024]{0:T(1024)} %constant.144) | copy-start | bytes 12292
  0.7 6.1 %copy-start.3 = (f32[10,512]{1,0:T(8,128)S(1)}, f32[10,512]{1,0:T(8,128)}, u32[]{:S(2)}) copy-start(f32[10,512]{1,0:T(8,128)} %constant.71) | copy-start | bytes 61444
  0.7 6.1 %copy-start.5 = (pred[10,512]{1,0:T(8,128)(4,1)S(1)}, pred[10,512]{1,0:T(8,128)(4,1)}, u32[]{:S(2)}) copy-start(pred[10,512]{1,0:T(8,128)(4,1)} %constant.59.clone) | copy-start | bytes 15364
  17.6 15.3 %collective-permute-start = (f32[4,512]{1,0:T(4,128)S(1)}, f32[4,512]{1,0:T(4,128)S(1)}, u32[]{:S(2)}, u32[]{:S(2)}) collective-permute-start(f32[4,512]{1,0:T(4,128)S(1)} %get-tuple-element.122), channel_id=1, source_target_pairs={{0,8},{8,0},{16,24},{24,16},{1,9},{9,1},{17,25},{25,17},{2,10},{10... | collective-permute-start | bytes 24584 | tf_op jit(solution)/shard_map/ppermute | solution.py:110
  20.7 12.2 %collective-permute-start.1 = (f32[4,512]{1,0:T(4,128)S(1)}, f32[4,512]{1,0:T(4,128)S(1)}, u32[]{:S(2)}, u32[]{:S(2)}) collective-permute-start(f32[4,512]{1,0:T(4,128)S(1)} %get-tuple-element.123), channel_id=1, source_target_pairs={{0,16},{8,24},{16,0},{24,8},{1,17},{9,25},{17,1},{25,9},{2,18},{10... | collective-permute-start | bytes 24584 | tf_op jit(solution)/shard_map/ppermute | solution.py:110
  23.3 9.6 %collective-permute-start.2 = (f32[4,512]{1,0:T(4,128)S(1)}, f32[4,512]{1,0:T(4,128)S(1)}, u32[]{:S(2)}, u32[]{:S(2)}) collective-permute-start(f32[4,512]{1,0:T(4,128)S(1)} %get-tuple-element.124), channel_id=1, source_target_pairs={{0,24},{8,16},{16,8},{24,0},{1,25},{9,17},{17,9},{25,1},{2,26},{10... | collective-permute-start | bytes 24584 | tf_op jit(solution)/shard_map/ppermute | solution.py:110
  34.4 3.7 %collective-permute-start.3 = (f32[4,1024]{1,0:T(4,128)S(1)}, f32[4,1024]{1,0:T(4,128)S(1)}, u32[]{:S(2)}, u32[]{:S(2)}) collective-permute-start(f32[4,1024]{1,0:T(4,128)S(1)} %get-tuple-element.130), channel_id=1, source_target_pairs={{0,1},{1,0},{2,3},{3,2},{4,5},{5,4},{6,7},{7,6},{8,9},{9,8},{10,11... | collective-permute-start | bytes 49160 | tf_op jit(solution)/shard_map/ppermute | solution.py:110
  34.4 6.2 %collective-permute-start.4 = (f32[4,1024]{1,0:T(4,128)S(1)}, f32[4,1024]{1,0:T(4,128)S(1)}, u32[]{:S(2)}, u32[]{:S(2)}) collective-permute-start(f32[4,1024]{1,0:T(4,128)S(1)} %get-tuple-element.131), channel_id=1, source_target_pairs={{0,2},{1,3},{2,0},{3,1},{4,6},{5,7},{6,4},{7,5},{8,10},{9,11},{10,... | collective-permute-start | bytes 49160 | tf_op jit(solution)/shard_map/ppermute | solution.py:110
  36.2 4.6 %collective-permute-start.5 = (f32[4,1024]{1,0:T(4,128)S(1)}, f32[4,1024]{1,0:T(4,128)S(1)}, u32[]{:S(2)}, u32[]{:S(2)}) collective-permute-start(f32[4,1024]{1,0:T(4,128)S(1)} %get-tuple-element.132), channel_id=1, source_target_pairs={{0,3},{1,2},{2,1},{3,0},{4,7},{5,6},{6,5},{7,4},{8,11},{9,10},{10,... | collective-permute-start | bytes 49160 | tf_op jit(solution)/shard_map/ppermute | solution.py:110
  36.3 4.5 %collective-permute-start.6 = (f32[4,1024]{1,0:T(4,128)S(1)}, f32[4,1024]{1,0:T(4,128)S(1)}, u32[]{:S(2)}, u32[]{:S(2)}) collective-permute-start(f32[4,1024]{1,0:T(4,128)S(1)} %get-tuple-element.133), channel_id=1, source_target_pairs={{0,4},{1,5},{2,6},{3,7},{4,0},{5,1},{6,2},{7,3},{8,12},{9,13},{10,... | collective-permute-start | bytes 49160 | tf_op jit(solution)/shard_map/ppermute | solution.py:110
  38.1 3.2 %collective-permute-start.7 = (f32[4,1024]{1,0:T(4,128)S(1)}, f32[4,1024]{1,0:T(4,128)S(1)}, u32[]{:S(2)}, u32[]{:S(2)}) collective-permute-start(f32[4,1024]{1,0:T(4,128)S(1)} %get-tuple-element.134), channel_id=1, source_target_pairs={{0,5},{1,4},{2,7},{3,6},{4,1},{5,0},{6,3},{7,2},{8,13},{9,12},{10,... | collective-permute-start | bytes 49160 | tf_op jit(solution)/shard_map/ppermute | solution.py:110
  38.1 4.7 %collective-permute-start.8 = (f32[4,1024]{1,0:T(4,128)S(1)}, f32[4,1024]{1,0:T(4,128)S(1)}, u32[]{:S(2)}, u32[]{:S(2)}) collective-permute-start(f32[4,1024]{1,0:T(4,128)S(1)} %get-tuple-element.135), channel_id=1, source_target_pairs={{0,6},{1,7},{2,4},{3,5},{4,2},{5,3},{6,0},{7,1},{8,14},{9,15},{10,... | collective-permute-start | bytes 49160 | tf_op jit(solution)/shard_map/ppermute | solution.py:110
  40.7 4.1 %collective-permute-start.9 = (f32[4,1024]{1,0:T(4,128)S(1)}, f32[4,1024]{1,0:T(4,128)S(1)}, u32[]{:S(2)}, u32[]{:S(2)}) collective-permute-start(f32[4,1024]{1,0:T(4,128)S(1)} %get-tuple-element.136), channel_id=1, source_target_pairs={{0,7},{1,6},{2,5},{3,4},{4,3},{5,2},{6,1},{7,0},{8,15},{9,14},{10,... | collective-permute-start | bytes 49160 | tf_op jit(solution)/shard_map/ppermute | solution.py:110
  54.0 14.2 %copy-start = (bf16[2,4,1024,256]{3,2,1,0:T(8,128)(2,1)}, bf16[2,4,1024,256]{3,2,1,0:T(8,128)(2,1)S(1)}, u32[]{:S(2)}) copy-start(bf16[2,4,1024,256]{3,2,1,0:T(8,128)(2,1)S(1)} %get-tuple-element.139.t_hi.refs_2_) | copy-start | bytes 12582916
  54.0 14.2 %copy-start.1 = (bf16[2,4,1024,256]{3,2,1,0:T(8,128)(2,1)}, bf16[2,4,1024,256]{3,2,1,0:T(8,128)(2,1)S(1)}, u32[]{:S(2)}) copy-start(bf16[2,4,1024,256]{3,2,1,0:T(8,128)(2,1)S(1)} %get-tuple-element.140.t_lo.refs_3_) | copy-start | bytes 12582916
  54.0 14.2 %collective-permute-start.10 = (f32[4,512]{1,0:T(4,128)S(1)}, f32[4,512]{1,0:T(4,128)S(1)}, u32[]{:S(2)}, u32[]{:S(2)}) collective-permute-start(f32[4,512]{1,0:T(4,128)S(1)} %get-tuple-element.145), channel_id=1, source_target_pairs={{0,8},{8,0},{16,24},{24,16},{1,9},{9,1},{17,25},{25,17},{2,10},{10... | collective-permute-start | bytes 24584 | tf_op jit(solution)/shard_map/ppermute | solution.py:110
  54.7 13.5 %collective-permute-start.11 = (f32[4,512]{1,0:T(4,128)S(1)}, f32[4,512]{1,0:T(4,128)S(1)}, u32[]{:S(2)}, u32[]{:S(2)}) collective-permute-start(f32[4,512]{1,0:T(4,128)S(1)} %get-tuple-element.146), channel_id=1, source_target_pairs={{0,16},{8,24},{16,0},{24,8},{1,17},{9,25},{17,1},{25,9},{2,18},{10... | collective-permute-start | bytes 24584 | tf_op jit(solution)/shard_map/ppermute | solution.py:110
  58.2 10.0 %collective-permute-start.12 = (f32[4,512]{1,0:T(4,128)S(1)}, f32[4,512]{1,0:T(4,128)S(1)}, u32[]{:S(2)}, u32[]{:S(2)}) collective-permute-start(f32[4,512]{1,0:T(4,128)S(1)} %get-tuple-element.147), channel_id=1, source_target_pairs={{0,24},{8,16},{16,8},{24,0},{1,25},{9,17},{17,9},{25,1},{2,26},{10... | collective-permute-start | bytes 24584 | tf_op jit(solution)/shard_map/ppermute | solution.py:110
  69.7 3.6 %collective-permute-start.13 = (f32[4,1024]{1,0:T(4,128)S(1)}, f32[4,1024]{1,0:T(4,128)S(1)}, u32[]{:S(2)}, u32[]{:S(2)}) collective-permute-start(f32[4,1024]{1,0:T(4,128)S(1)} %get-tuple-element.151), channel_id=1, source_target_pairs={{0,1},{1,0},{2,3},{3,2},{4,5},{5,4},{6,7},{7,6},{8,9},{9,8},{10,11... | collective-permute-start | bytes 49160 | tf_op jit(solution)/shard_map/ppermute | solution.py:110
  69.7 4.1 %collective-permute-start.14 = (f32[4,1024]{1,0:T(4,128)S(1)}, f32[4,1024]{1,0:T(4,128)S(1)}, u32[]{:S(2)}, u32[]{:S(2)}) collective-permute-start(f32[4,1024]{1,0:T(4,128)S(1)} %get-tuple-element.152), channel_id=1, source_target_pairs={{0,2},{1,3},{2,0},{3,1},{4,6},{5,7},{6,4},{7,5},{8,10},{9,11},{10,... | collective-permute-start | bytes 49160 | tf_op jit(solution)/shard_map/ppermute | solution.py:110
  70.3 5.7 %collective-permute-start.15 = (f32[4,1024]{1,0:T(4,128)S(1)}, f32[4,1024]{1,0:T(4,128)S(1)}, u32[]{:S(2)}, u32[]{:S(2)}) collective-permute-start(f32[4,1024]{1,0:T(4,128)S(1)} %get-tuple-element.153), channel_id=1, source_target_pairs={{0,3},{1,2},{2,1},{3,0},{4,7},{5,6},{6,5},{7,4},{8,11},{9,10},{10,... | collective-permute-start | bytes 49160 | tf_op jit(solution)/shard_map/ppermute | solution.py:110
  71.6 4.4 %collective-permute-start.16 = (f32[4,1024]{1,0:T(4,128)S(1)}, f32[4,1024]{1,0:T(4,128)S(1)}, u32[]{:S(2)}, u32[]{:S(2)}) collective-permute-start(f32[4,1024]{1,0:T(4,128)S(1)} %get-tuple-element.154), channel_id=1, source_target_pairs={{0,4},{1,5},{2,6},{3,7},{4,0},{5,1},{6,2},{7,3},{8,12},{9,13},{10,... | collective-permute-start | bytes 49160 | tf_op jit(solution)/shard_map/ppermute | solution.py:110
  72.1 3.9 %collective-permute-start.17 = (f32[4,1024]{1,0:T(4,128)S(1)}, f32[4,1024]{1,0:T(4,128)S(1)}, u32[]{:S(2)}, u32[]{:S(2)}) collective-permute-start(f32[4,1024]{1,0:T(4,128)S(1)} %get-tuple-element.155), channel_id=1, source_target_pairs={{0,5},{1,4},{2,7},{3,6},{4,1},{5,0},{6,3},{7,2},{8,13},{9,12},{10,... | collective-permute-start | bytes 49160 | tf_op jit(solution)/shard_map/ppermute | solution.py:110
  73.3 4.8 %collective-permute-start.18 = (f32[4,1024]{1,0:T(4,128)S(1)}, f32[4,1024]{1,0:T(4,128)S(1)}, u32[]{:S(2)}, u32[]{:S(2)}) collective-permute-start(f32[4,1024]{1,0:T(4,128)S(1)} %get-tuple-element.156), channel_id=1, source_target_pairs={{0,6},{1,7},{2,4},{3,5},{4,2},{5,3},{6,0},{7,1},{8,14},{9,15},{10,... | collective-permute-start | bytes 49160 | tf_op jit(solution)/shard_map/ppermute | solution.py:110
  73.9 4.2 %collective-permute-start.19 = (f32[4,1024]{1,0:T(4,128)S(1)}, f32[4,1024]{1,0:T(4,128)S(1)}, u32[]{:S(2)}, u32[]{:S(2)}) collective-permute-start(f32[4,1024]{1,0:T(4,128)S(1)} %get-tuple-element.157), channel_id=1, source_target_pairs={{0,7},{1,6},{2,5},{3,4},{4,3},{5,2},{6,1},{7,0},{8,15},{9,14},{10,... | collective-permute-start | bytes 49160 | tf_op jit(solution)/shard_map/ppermute | solution.py:110
  87.1 14.3 %collective-permute-start.20 = (f32[4,512]{1,0:T(4,128)S(1)}, f32[4,512]{1,0:T(4,128)S(1)}, u32[]{:S(2)}, u32[]{:S(2)}) collective-permute-start(f32[4,512]{1,0:T(4,128)S(1)} %get-tuple-element.167), channel_id=1, source_target_pairs={{0,8},{8,0},{16,24},{24,16},{1,9},{9,1},{17,25},{25,17},{2,10},{10... | collective-permute-start | bytes 24584 | tf_op jit(solution)/shard_map/ppermute | solution.py:110
  87.6 13.9 %collective-permute-start.21 = (f32[4,512]{1,0:T(4,128)S(1)}, f32[4,512]{1,0:T(4,128)S(1)}, u32[]{:S(2)}, u32[]{:S(2)}) collective-permute-start(f32[4,512]{1,0:T(4,128)S(1)} %get-tuple-element.168), channel_id=1, source_target_pairs={{0,16},{8,24},{16,0},{24,8},{1,17},{9,25},{17,1},{25,9},{2,18},{10... | collective-permute-start | bytes 24584 | tf_op jit(solution)/shard_map/ppermute | solution.py:110
  91.4 10.1 %collective-permute-start.22 = (f32[4,512]{1,0:T(4,128)S(1)}, f32[4,512]{1,0:T(4,128)S(1)}, u32[]{:S(2)}, u32[]{:S(2)}) collective-permute-start(f32[4,512]{1,0:T(4,128)S(1)} %get-tuple-element.169), channel_id=1, source_target_pairs={{0,24},{8,16},{16,8},{24,0},{1,25},{9,17},{17,9},{25,1},{2,26},{10... | collective-permute-start | bytes 24584 | tf_op jit(solution)/shard_map/ppermute | solution.py:110
  102.9 3.6 %collective-permute-start.23 = (f32[4,1024]{1,0:T(4,128)S(1)}, f32[4,1024]{1,0:T(4,128)S(1)}, u32[]{:S(2)}, u32[]{:S(2)}) collective-permute-start(f32[4,1024]{1,0:T(4,128)S(1)} %get-tuple-element.173), channel_id=1, source_target_pairs={{0,1},{1,0},{2,3},{3,2},{4,5},{5,4},{6,7},{7,6},{8,9},{9,8},{10,11... | collective-permute-start | bytes 49160 | tf_op jit(solution)/shard_map/ppermute | solution.py:110
  103.0 5.8 %collective-permute-start.24 = (f32[4,1024]{1,0:T(4,128)S(1)}, f32[4,1024]{1,0:T(4,128)S(1)}, u32[]{:S(2)}, u32[]{:S(2)}) collective-permute-start(f32[4,1024]{1,0:T(4,128)S(1)} %get-tuple-element.174), channel_id=1, source_target_pairs={{0,2},{1,3},{2,0},{3,1},{4,6},{5,7},{6,4},{7,5},{8,10},{9,11},{10,... | collective-permute-start | bytes 49160 | tf_op jit(solution)/shard_map/ppermute | solution.py:110
  104.2 5.0 %collective-permute-start.25 = (f32[4,1024]{1,0:T(4,128)S(1)}, f32[4,1024]{1,0:T(4,128)S(1)}, u32[]{:S(2)}, u32[]{:S(2)}) collective-permute-start(f32[4,1024]{1,0:T(4,128)S(1)} %get-tuple-element.175), channel_id=1, source_target_pairs={{0,3},{1,2},{2,1},{3,0},{4,7},{5,6},{6,5},{7,4},{8,11},{9,10},{10,... | collective-permute-start | bytes 49160 | tf_op jit(solution)/shard_map/ppermute | solution.py:110
  104.8 4.4 %collective-permute-start.26 = (f32[4,1024]{1,0:T(4,128)S(1)}, f32[4,1024]{1,0:T(4,128)S(1)}, u32[]{:S(2)}, u32[]{:S(2)}) collective-permute-start(f32[4,1024]{1,0:T(4,128)S(1)} %get-tuple-element.176), channel_id=1, source_target_pairs={{0,4},{1,5},{2,6},{3,7},{4,0},{5,1},{6,2},{7,3},{8,12},{9,13},{10,... | collective-permute-start | bytes 49160 | tf_op jit(solution)/shard_map/ppermute | solution.py:110
  106.1 3.2 %collective-permute-start.27 = (f32[4,1024]{1,0:T(4,128)S(1)}, f32[4,1024]{1,0:T(4,128)S(1)}, u32[]{:S(2)}, u32[]{:S(2)}) collective-permute-start(f32[4,1024]{1,0:T(4,128)S(1)} %get-tuple-element.177), channel_id=1, source_target_pairs={{0,5},{1,4},{2,7},{3,6},{4,1},{5,0},{6,3},{7,2},{8,13},{9,12},{10,... | collective-permute-start | bytes 49160 | tf_op jit(solution)/shard_map/ppermute | solution.py:110
  106.5 4.6 %collective-permute-start.28 = (f32[4,1024]{1,0:T(4,128)S(1)}, f32[4,1024]{1,0:T(4,128)S(1)}, u32[]{:S(2)}, u32[]{:S(2)}) collective-permute-start(f32[4,1024]{1,0:T(4,128)S(1)} %get-tuple-element.178), channel_id=1, source_target_pairs={{0,6},{1,7},{2,4},{3,5},{4,2},{5,3},{6,0},{7,1},{8,14},{9,15},{10,... | collective-permute-start | bytes 49160 | tf_op jit(solution)/shard_map/ppermute | solution.py:110
  108.7 4.1 %collective-permute-start.29 = (f32[4,1024]{1,0:T(4,128)S(1)}, f32[4,1024]{1,0:T(4,128)S(1)}, u32[]{:S(2)}, u32[]{:S(2)}) collective-permute-start(f32[4,1024]{1,0:T(4,128)S(1)} %get-tuple-element.179), channel_id=1, source_target_pairs={{0,7},{1,6},{2,5},{3,4},{4,3},{5,2},{6,1},{7,0},{8,15},{9,14},{10,... | collective-permute-start | bytes 49160 | tf_op jit(solution)/shard_map/ppermute | solution.py:110
  122.5 14.3 %collective-permute-start.30 = (f32[4,512]{1,0:T(4,128)S(1)}, f32[4,512]{1,0:T(4,128)S(1)}, u32[]{:S(2)}, u32[]{:S(2)}) collective-permute-start(f32[4,512]{1,0:T(4,128)S(1)} %get-tuple-element.192), channel_id=1, source_target_pairs={{0,8},{8,0},{16,24},{24,16},{1,9},{9,1},{17,25},{25,17},{2,10},{10... | collective-permute-start | bytes 24584 | tf_op jit(solution)/shard_map/ppermute | solution.py:110
  122.9 13.9 %collective-permute-start.31 = (f32[4,512]{1,0:T(4,128)S(1)}, f32[4,512]{1,0:T(4,128)S(1)}, u32[]{:S(2)}, u32[]{:S(2)}) collective-permute-start(f32[4,512]{1,0:T(4,128)S(1)} %get-tuple-element.193), channel_id=1, source_target_pairs={{0,16},{8,24},{16,0},{24,8},{1,17},{9,25},{17,1},{25,9},{2,18},{10... | collective-permute-start | bytes 24584 | tf_op jit(solution)/shard_map/ppermute | solution.py:110
  126.7 10.1 %collective-permute-start.32 = (f32[4,512]{1,0:T(4,128)S(1)}, f32[4,512]{1,0:T(4,128)S(1)}, u32[]{:S(2)}, u32[]{:S(2)}) collective-permute-start(f32[4,512]{1,0:T(4,128)S(1)} %get-tuple-element.194), channel_id=1, source_target_pairs={{0,24},{8,16},{16,8},{24,0},{1,25},{9,17},{17,9},{25,1},{2,26},{10... | collective-permute-start | bytes 24584 | tf_op jit(solution)/shard_map/ppermute | solution.py:110
  138.2 3.6 %collective-permute-start.33 = (f32[4,1024]{1,0:T(4,128)S(1)}, f32[4,1024]{1,0:T(4,128)S(1)}, u32[]{:S(2)}, u32[]{:S(2)}) collective-permute-start(f32[4,1024]{1,0:T(4,128)S(1)} %get-tuple-element.198), channel_id=1, source_target_pairs={{0,1},{1,0},{2,3},{3,2},{4,5},{5,4},{6,7},{7,6},{8,9},{9,8},{10,11... | collective-permute-start | bytes 49160 | tf_op jit(solution)/shard_map/ppermute | solution.py:110
  138.3 4.3 %collective-permute-start.34 = (f32[4,1024]{1,0:T(4,128)S(1)}, f32[4,1024]{1,0:T(4,128)S(1)}, u32[]{:S(2)}, u32[]{:S(2)}) collective-permute-start(f32[4,1024]{1,0:T(4,128)S(1)} %get-tuple-element.199), channel_id=1, source_target_pairs={{0,2},{1,3},{2,0},{3,1},{4,6},{5,7},{6,4},{7,5},{8,10},{9,11},{10,... | collective-permute-start | bytes 49160 | tf_op jit(solution)/shard_map/ppermute | solution.py:110
  138.9 5.7 %collective-permute-start.35 = (f32[4,1024]{1,0:T(4,128)S(1)}, f32[4,1024]{1,0:T(4,128)S(1)}, u32[]{:S(2)}, u32[]{:S(2)}) collective-permute-start(f32[4,1024]{1,0:T(4,128)S(1)} %get-tuple-element.200), channel_id=1, source_target_pairs={{0,3},{1,2},{2,1},{3,0},{4,7},{5,6},{6,5},{7,4},{8,11},{9,10},{10,... | collective-permute-start | bytes 49160 | tf_op jit(solution)/shard_map/ppermute | solution.py:110
  140.2 4.4 %collective-permute-start.36 = (f32[4,1024]{1,0:T(4,128)S(1)}, f32[4,1024]{1,0:T(4,128)S(1)}, u32[]{:S(2)}, u32[]{:S(2)}) collective-permute-start(f32[4,1024]{1,0:T(4,128)S(1)} %get-tuple-element.201), channel_id=1, source_target_pairs={{0,4},{1,5},{2,6},{3,7},{4,0},{5,1},{6,2},{7,3},{8,12},{9,13},{10,... | collective-permute-start | bytes 49160 | tf_op jit(solution)/shard_map/ppermute | solution.py:110
  140.7 3.9 %collective-permute-start.37 = (f32[4,1024]{1,0:T(4,128)S(1)}, f32[4,1024]{1,0:T(4,128)S(1)}, u32[]{:S(2)}, u32[]{:S(2)}) collective-permute-start(f32[4,1024]{1,0:T(4,128)S(1)} %get-tuple-element.202), channel_id=1, source_target_pairs={{0,5},{1,4},{2,7},{3,6},{4,1},{5,0},{6,3},{7,2},{8,13},{9,12},{10,... | collective-permute-start | bytes 49160 | tf_op jit(solution)/shard_map/ppermute | solution.py:110
  141.9 4.6 %collective-permute-start.38 = (f32[4,1024]{1,0:T(4,128)S(1)}, f32[4,1024]{1,0:T(4,128)S(1)}, u32[]{:S(2)}, u32[]{:S(2)}) collective-permute-start(f32[4,1024]{1,0:T(4,128)S(1)} %get-tuple-element.203), channel_id=1, source_target_pairs={{0,6},{1,7},{2,4},{3,5},{4,2},{5,3},{6,0},{7,1},{8,14},{9,15},{10,... | collective-permute-start | bytes 49160 | tf_op jit(solution)/shard_map/ppermute | solution.py:110
  142.6 4.1 %collective-permute-start.39 = (f32[4,1024]{1,0:T(4,128)S(1)}, f32[4,1024]{1,0:T(4,128)S(1)}, u32[]{:S(2)}, u32[]{:S(2)}) collective-permute-start(f32[4,1024]{1,0:T(4,128)S(1)} %get-tuple-element.204), channel_id=1, source_target_pairs={{0,7},{1,6},{2,5},{3,4},{4,3},{5,2},{6,1},{7,0},{8,15},{9,14},{10,... | collective-permute-start | bytes 49160 | tf_op jit(solution)/shard_map/ppermute | solution.py:110
  (9 other events, 13.0 us)
